TPU v7x, 512 devices: a whole 4x4x16 slice. The times are simulated.
512 devices in a mesh: blk: 16 (over x, y_hi, core), dp: 32 (over z, y_lo).
Axes of the slice: x: 4, y: 4 (y_hi: 2, y_lo: 2; y = y_hi * 2 + y_lo), z: 16, core: 2. Of those that a mesh axis runs over, the one named last changes fastest.
Arguments:
- inputs: bfloat16 [65536, 5120], P(('blk', 'dp')), may hold values from -400 to 400
- queries: bfloat16 [65536, 2560], P(('blk', 'dp')), may hold values from -96 to 96
- keys: bfloat16 [65536, 512], P(('blk', 'dp')), may hold values from -4 to 4
- doc_ids: int32 [65536], P(('blk', 'dp')), may hold values from 0 to 65535, as said below
- grad_out: bfloat16 [65536, 2560], P(('blk', 'dp')), may hold values from -6 to 6
- gain: float32 [5120], replicated, may hold values from 0.25 to 1.75
- bias: float32 [512], replicated, may hold values from -3 to 3
- w_value: bfloat16 [5120, 512], P('blk'), may hold values from -0.078125 to 0.078125
Outputs:
- attention: bfloat16 [65536, 2560], P(('blk', 'dp'))
- grad_inputs: bfloat16 [65536, 5120], P(('blk', 'dp'))
- grad_w_value: float32 [5120, 512], P('blk', 'dp')
- grad_gain: float32 [5120], replicated
- grad_bias: float32 [512], replicated
Inputs may be any that keep to these rules, and one draw needn't show every extreme that they name: `doc_ids`: document ids never fall along the tokens; the first token has id 0 and the last token alone has id 65536 - 1.
All inputs are finite; a program needn't handle non-finite values.
Results may differ from a plain program's by a relative error of at most 0.012.
Values may be sent and summed in bfloat16 or wider, within the bound.
A program may use at most 64 MiB of HBM per device.

v0:
```python
import math

import jax
import jax.numpy as jnp
from jax import lax
from jax.sharding import PartitionSpec as P

HD = 128


def passed_along(shard, axis, by):
    devices = lax.axis_size(axis)
    return lax.ppermute(shard, axis, [(i, (i + by) % devices) for i in range(devices)])


def norm_forward(inputs, gain):
    values = inputs.astype(jnp.float32)
    inverse_rms = lax.rsqrt(jnp.mean(values * values, axis=-1, keepdims=True) + 1e-06)
    normed = values * inverse_rms
    return (normed, inverse_rms, (normed * gain).astype(jnp.bfloat16))


def attend(queries, keys, doc_ids, value_rows, grad_rows):
    row_count = queries.shape[0]
    kv_heads = keys.shape[1] // HD
    group_size = queries.shape[1] // keys.shape[1]
    query_heads = queries.reshape(row_count, kv_heads, group_size, HD)
    key_heads = keys.reshape(row_count, kv_heads, HD)
    scores = jnp.einsum(
        "qgjd,kgd->gjqk", query_heads, key_heads, preferred_element_type=jnp.float32
    ) * (1.0 / math.sqrt(HD))
    positions = jnp.arange(row_count)
    allowed = (positions[:, None] >= positions[None, :]) & (doc_ids[:, None] == doc_ids[None, :])
    scores = jnp.where(allowed, scores, -1e30)
    row_max = jnp.max(scores, axis=-1, keepdims=True)
    exponent = jnp.exp(scores - row_max)
    probabilities = (exponent / jnp.sum(exponent, axis=-1, keepdims=True)).astype(jnp.bfloat16)
    value_heads = value_rows.reshape(row_count, kv_heads, HD)
    attention = jnp.einsum(
        "gjqk,kgd->qgjd", probabilities, value_heads, preferred_element_type=jnp.float32
    )
    attention = attention.reshape(row_count, queries.shape[1]).astype(jnp.bfloat16)
    grad_heads = grad_rows.reshape(row_count, kv_heads, group_size, HD)
    value_grad = jnp.einsum(
        "gjqk,qgjd->kgd", probabilities, grad_heads, preferred_element_type=jnp.float32
    )
    return (attention, value_grad.reshape(row_count, keys.shape[1]))


def local(inputs, queries, keys, doc_ids, grad_out, gain, bias, w_value):
    cycle_size = lax.axis_size("blk")
    my_index = lax.axis_index("blk")
    row_count = inputs.shape[0]
    share_rows = w_value.shape[0]
    kv_width = w_value.shape[1]
    normed, inverse_rms, hidden = norm_forward(inputs, gain)
    weight_piece = lax.all_gather(w_value, "blk", axis=0, tiled=True)
    running = jnp.zeros((row_count, kv_width), jnp.float32)
    hidden_cols = hidden
    running = jnp.dot(hidden_cols, weight_piece, preferred_element_type=jnp.float32)
    value_sum = running
    value = (value_sum + bias).astype(jnp.bfloat16)
    attention, value_grad = attend(queries, keys, doc_ids, value, grad_out)
    value_grad_b = value_grad.astype(jnp.bfloat16)
    hidden_grad = lax.dot_general(
        value_grad_b, weight_piece, (((1,), (1,)), ((), ())), preferred_element_type=jnp.float32
    ).astype(jnp.bfloat16)

    def contribution(block_index):
        hidden_cols = lax.dynamic_slice_in_dim(hidden, block_index * share_rows, share_rows, 1)
        return lax.dot_general(
            hidden_cols, value_grad_b, (((0,), (0,)), ((), ())), preferred_element_type=jnp.float32
        )

    def cycle_step(turn_index, running):
        running = passed_along(running, "blk", 1)
        return running + contribution((my_index + 2 * cycle_size - turn_index - 1) % cycle_size)

    weight_block = contribution((my_index + cycle_size - 1) % cycle_size)
    weight_block = lax.fori_loop(1, cycle_size, cycle_step, weight_block)
    replica_count = lax.axis_size("dp")
    grad_w_value = (
        lax.psum_scatter(weight_block, "dp", scatter_dimension=1, tiled=True) / replica_count
    )
    hidden_wide = hidden_grad.astype(jnp.float32)
    gain_term = jnp.sum(hidden_wide * normed, axis=0)
    bias_term = jnp.sum(value_grad, axis=0)
    gain_total, bias_total = lax.psum((gain_term, bias_term), ("blk", "dp"))
    normed_grad = hidden_wide * gain
    grad_inputs = (
        inverse_rms
        * (normed_grad - normed * jnp.mean(normed_grad * normed, axis=-1, keepdims=True))
    ).astype(jnp.bfloat16)
    return (
        attention,
        grad_inputs,
        grad_w_value,
        gain_total / replica_count,
        bias_total / replica_count,
    )


def solution(mesh):
    placed = (
        P(("blk", "dp"), None),
        P(("blk", "dp"), None),
        P(("blk", "dp"), None),
        P(("blk", "dp")),
        P(("blk", "dp"), None),
        P(),
        P(),
        P("blk", None),
    )
    return jax.shard_map(
        local,
        mesh=mesh,
        in_specs=placed,
        out_specs=(P(("blk", "dp"), None), P(("blk", "dp"), None), P("blk", "dp"), P(), P()),
        check_vma=False,
    )
```

profile of v0, /device:TPU:6, one launch (start us, length us, event | category | flops | bytes accessed | tf_op | source)
XLA Modules:
  0.0 478.1 jit_solution(6389870331631367758)
XLA Ops:
  13.9 76.8 %all-gather.2.cloned.1.call-done = bf16[5120,512]{1,0:T(8,128)(2,1)} async-done(((bf16[320,512]{1,0:T(8,128)(2,1)}), bf16[5120,512]{1,0:T(8,128)(2,1)}) %all-gather.2.cloned.1.call-update) | async-done | bytes 5242896 | tf_op jit(solution)/shard_map/all_gather | solution.py:57
  90.8 4.7 fusion.13
  97.7 220.0 %while.15 = (s32[]{:T(128)}, f32[320,512]{1,0:T(8,128)S(1)}, s32[]{:T(128)}, bf16[128,5120]{1,0:T(8,128)(2,1)S(1)}, bf16[128,512]{1,0:T(8,128)(2,1)S(1)}, /*inde...) while((s32[]{:T(128)}, f32[320,512]{1,0:T(8,128)S(1)}, ...), condition=%wide.region_5.6_spmd, body=%wide.region_4.5_spmd.sunk | while | flops 42106896 | bytes 4161876 | solution.py:80
  97.7 2.1 collective-permute-start
  99.9 12.1 %collective-permute-done = f32[320,512]{1,0:T(8,128)S(1)} collective-permute-done((f32[320,512]{1,0:T(8,128)S(1)}, f32[320,512]{1,0:T(8,128)S(1)}, u32[]{:S(2)}, u32[]{:S(2)}) %collective-permute-start) | collective-permute-done | bytes 655392 | tf_op jit(solution)/shard_map/while/body/eval_jaxpr/ppermute | solution.py:13
  114.3 12.4 %collective-permute-done = f32[320,512]{1,0:T(8,128)S(1)} collective-permute-done((f32[320,512]{1,0:T(8,128)S(1)}, f32[320,512]{1,0:T(8,128)S(1)}, u32[]{:S(2)}, u32[]{:S(2)}) %collective-permute-start) | collective-permute-done | bytes 655392 | tf_op jit(solution)/shard_map/while/body/eval_jaxpr/ppermute | solution.py:13
  127.1 1.9 collective-permute-start
  129.0 12.4 %collective-permute-done = f32[320,512]{1,0:T(8,128)S(1)} collective-permute-done((f32[320,512]{1,0:T(8,128)S(1)}, f32[320,512]{1,0:T(8,128)S(1)}, u32[]{:S(2)}, u32[]{:S(2)}) %collective-permute-start) | collective-permute-done | bytes 655392 | tf_op jit(solution)/shard_map/while/body/eval_jaxpr/ppermute | solution.py:13
  141.7 1.9 collective-permute-start
  143.7 12.4 %collective-permute-done = f32[320,512]{1,0:T(8,128)S(1)} collective-permute-done((f32[320,512]{1,0:T(8,128)S(1)}, f32[320,512]{1,0:T(8,128)S(1)}, u32[]{:S(2)}, u32[]{:S(2)}) %collective-permute-start) | collective-permute-done | bytes 655392 | tf_op jit(solution)/shard_map/while/body/eval_jaxpr/ppermute | solution.py:13
  158.4 12.4 %collective-permute-done = f32[320,512]{1,0:T(8,128)S(1)} collective-permute-done((f32[320,512]{1,0:T(8,128)S(1)}, f32[320,512]{1,0:T(8,128)S(1)}, u32[]{:S(2)}, u32[]{:S(2)}) %collective-permute-start) | collective-permute-done | bytes 655392 | tf_op jit(solution)/shard_map/while/body/eval_jaxpr/ppermute | solution.py:13
  173.0 12.4 %collective-permute-done = f32[320,512]{1,0:T(8,128)S(1)} collective-permute-done((f32[320,512]{1,0:T(8,128)S(1)}, f32[320,512]{1,0:T(8,128)S(1)}, u32[]{:S(2)}, u32[]{:S(2)}) %collective-permute-start) | collective-permute-done | bytes 655392 | tf_op jit(solution)/shard_map/while/body/eval_jaxpr/ppermute | solution.py:13
  187.7 12.4 %collective-permute-done = f32[320,512]{1,0:T(8,128)S(1)} collective-permute-done((f32[320,512]{1,0:T(8,128)S(1)}, f32[320,512]{1,0:T(8,128)S(1)}, u32[]{:S(2)}, u32[]{:S(2)}) %collective-permute-start) | collective-permute-done | bytes 655392 | tf_op jit(solution)/shard_map/while/body/eval_jaxpr/ppermute | solution.py:13
  202.4 12.4 %collective-permute-done = f32[320,512]{1,0:T(8,128)S(1)} collective-permute-done((f32[320,512]{1,0:T(8,128)S(1)}, f32[320,512]{1,0:T(8,128)S(1)}, u32[]{:S(2)}, u32[]{:S(2)}) %collective-permute-start) | collective-permute-done | bytes 655392 | tf_op jit(solution)/shard_map/while/body/eval_jaxpr/ppermute | solution.py:13
  217.0 12.4 %collective-permute-done = f32[320,512]{1,0:T(8,128)S(1)} collective-permute-done((f32[320,512]{1,0:T(8,128)S(1)}, f32[320,512]{1,0:T(8,128)S(1)}, u32[]{:S(2)}, u32[]{:S(2)}) %collective-permute-start) | collective-permute-done | bytes 655392 | tf_op jit(solution)/shard_map/while/body/eval_jaxpr/ppermute | solution.py:13
  231.7 12.4 %collective-permute-done = f32[320,512]{1,0:T(8,128)S(1)} collective-permute-done((f32[320,512]{1,0:T(8,128)S(1)}, f32[320,512]{1,0:T(8,128)S(1)}, u32[]{:S(2)}, u32[]{:S(2)}) %collective-permute-start) | collective-permute-done | bytes 655392 | tf_op jit(solution)/shard_map/while/body/eval_jaxpr/ppermute | solution.py:13
  246.4 12.4 %collective-permute-done = f32[320,512]{1,0:T(8,128)S(1)} collective-permute-done((f32[320,512]{1,0:T(8,128)S(1)}, f32[320,512]{1,0:T(8,128)S(1)}, u32[]{:S(2)}, u32[]{:S(2)}) %collective-permute-start) | collective-permute-done | bytes 655392 | tf_op jit(solution)/shard_map/while/body/eval_jaxpr/ppermute | solution.py:13
  261.0 12.4 %collective-permute-done = f32[320,512]{1,0:T(8,128)S(1)} collective-permute-done((f32[320,512]{1,0:T(8,128)S(1)}, f32[320,512]{1,0:T(8,128)S(1)}, u32[]{:S(2)}, u32[]{:S(2)}) %collective-permute-start) | collective-permute-done | bytes 655392 | tf_op jit(solution)/shard_map/while/body/eval_jaxpr/ppermute | solution.py:13
  275.7 12.4 %collective-permute-done = f32[320,512]{1,0:T(8,128)S(1)} collective-permute-done((f32[320,512]{1,0:T(8,128)S(1)}, f32[320,512]{1,0:T(8,128)S(1)}, u32[]{:S(2)}, u32[]{:S(2)}) %collective-permute-start) | collective-permute-done | bytes 655392 | tf_op jit(solution)/shard_map/while/body/eval_jaxpr/ppermute | solution.py:13
  290.4 12.4 %collective-permute-done = f32[320,512]{1,0:T(8,128)S(1)} collective-permute-done((f32[320,512]{1,0:T(8,128)S(1)}, f32[320,512]{1,0:T(8,128)S(1)}, u32[]{:S(2)}, u32[]{:S(2)}) %collective-permute-start) | collective-permute-done | bytes 655392 | tf_op jit(solution)/shard_map/while/body/eval_jaxpr/ppermute | solution.py:13
  305.0 12.4 %collective-permute-done = f32[320,512]{1,0:T(8,128)S(1)} collective-permute-done((f32[320,512]{1,0:T(8,128)S(1)}, f32[320,512]{1,0:T(8,128)S(1)}, u32[]{:S(2)}, u32[]{:S(2)}) %collective-permute-start) | collective-permute-done | bytes 655392 | tf_op jit(solution)/shard_map/while/body/eval_jaxpr/ppermute | solution.py:13
  319.0 3.3 fusion.19
  325.2 120.5 %all-reduce = (f32[5120]{0:T(1024)S(1)}, f32[512]{0:T(512)S(1)}) all-reduce(f32[5120]{0:T(1024)S(1)} %get-tuple-element.162, f32[512]{0:T(512)S(1)} %bitcast.47), channel_id=1, replica_groups=mesh['blk'=16,'dp'=32] {'blk','dp'}, use_global_device_ids=true, to_apply=%region_8.9 | all-reduce | flops 5632 | bytes 45056 | tf_op jit(solution)/shard_map/psum | solution.py:88
  446.8 23.1 %reduce-scatter.2.cloned.1.call-done = f32[320,16]{0,1:T(8,128)} async-done(((f32[320,512]{0,1:T(8,128)}), f32[320,16]{0,1:T(8,128)}) %reduce-scatter.2.cloned.1.call-update) | async-done | bytes 20496 | tf_op jit(solution)/shard_map/reduce_scatter | solution.py:83
  (62 shorter events, 43.6 us)
Async XLA Ops:
  7.2 2.3 copy-start.1
  7.2 83.6 %all-gather.2.cloned.1.call-start = ((), (), s32[]{:S(2)}) async-start(), calls=%async_computation.1 | async-start | bytes 5570560 | tf_op jit(solution)/shard_map/all_gather | solution.py:57
  7.9 462.0 %reduce-scatter.2.cloned.1.call-start = ((), (), s32[]{:S(2)}) async-start(), calls=%async_computation.2 | async-start | bytes 811008 | tf_op jit(solution)/shard_map/reduce_scatter | solution.py:83
  8.0 1.8 copy-start.2
  8.0 1.9 copy-start.5
  11.6 2.0 copy-start
  13.5 77.3 %copy-start.3 = (f32[5120]{0:T(1024)S(1)}, f32[5120]{0:T(1024)}, u32[]{:S(2)}) copy-start(f32[5120]{0:T(1024)} %param.15) | copy-start | bytes 61444
  97.7 14.3 %collective-permute-start = (f32[320,512]{1,0:T(8,128)S(1)}, f32[320,512]{1,0:T(8,128)S(1)}, u32[]{:S(2)}, u32[]{:S(2)}) collective-permute-start(f32[320,512]{1,0:T(8,128)S(1)} %get-tuple-element.228), channel_id=1, source_target_pairs={{0,32},{32,64},{64,96},{96,128},{128,160},{160,192},{192,224},{224... | collective-permute-start | bytes 1966088 | tf_op jit(solution)/shard_map/while/body/eval_jaxpr/ppermute | solution.py:13
  112.4 14.3 %collective-permute-start = (f32[320,512]{1,0:T(8,128)S(1)}, f32[320,512]{1,0:T(8,128)S(1)}, u32[]{:S(2)}, u32[]{:S(2)}) collective-permute-start(f32[320,512]{1,0:T(8,128)S(1)} %get-tuple-element.228), channel_id=1, source_target_pairs={{0,32},{32,64},{64,96},{96,128},{128,160},{160,192},{192,224},{224... | collective-permute-start | bytes 1966088 | tf_op jit(solution)/shard_map/while/body/eval_jaxpr/ppermute | solution.py:13
  127.1 14.3 %collective-permute-start = (f32[320,512]{1,0:T(8,128)S(1)}, f32[320,512]{1,0:T(8,128)S(1)}, u32[]{:S(2)}, u32[]{:S(2)}) collective-permute-start(f32[320,512]{1,0:T(8,128)S(1)} %get-tuple-element.228), channel_id=1, source_target_pairs={{0,32},{32,64},{64,96},{96,128},{128,160},{160,192},{192,224},{224... | collective-permute-start | bytes 1966088 | tf_op jit(solution)/shard_map/while/body/eval_jaxpr/ppermute | solution.py:13
  141.7 14.3 %collective-permute-start = (f32[320,512]{1,0:T(8,128)S(1)}, f32[320,512]{1,0:T(8,128)S(1)}, u32[]{:S(2)}, u32[]{:S(2)}) collective-permute-start(f32[320,512]{1,0:T(8,128)S(1)} %get-tuple-element.228), channel_id=1, source_target_pairs={{0,32},{32,64},{64,96},{96,128},{128,160},{160,192},{192,224},{224... | collective-permute-start | bytes 1966088 | tf_op jit(solution)/shard_map/while/body/eval_jaxpr/ppermute | solution.py:13
  156.4 14.3 %collective-permute-start = (f32[320,512]{1,0:T(8,128)S(1)}, f32[320,512]{1,0:T(8,128)S(1)}, u32[]{:S(2)}, u32[]{:S(2)}) collective-permute-start(f32[320,512]{1,0:T(8,128)S(1)} %get-tuple-element.228), channel_id=1, source_target_pairs={{0,32},{32,64},{64,96},{96,128},{128,160},{160,192},{192,224},{224... | collective-permute-start | bytes 1966088 | tf_op jit(solution)/shard_map/while/body/eval_jaxpr/ppermute | solution.py:13
  171.1 14.3 %collective-permute-start = (f32[320,512]{1,0:T(8,128)S(1)}, f32[320,512]{1,0:T(8,128)S(1)}, u32[]{:S(2)}, u32[]{:S(2)}) collective-permute-start(f32[320,512]{1,0:T(8,128)S(1)} %get-tuple-element.228), channel_id=1, source_target_pairs={{0,32},{32,64},{64,96},{96,128},{128,160},{160,192},{192,224},{224... | collective-permute-start | bytes 1966088 | tf_op jit(solution)/shard_map/while/body/eval_jaxpr/ppermute | solution.py:13
  185.7 14.3 %collective-permute-start = (f32[320,512]{1,0:T(8,128)S(1)}, f32[320,512]{1,0:T(8,128)S(1)}, u32[]{:S(2)}, u32[]{:S(2)}) collective-permute-start(f32[320,512]{1,0:T(8,128)S(1)} %get-tuple-element.228), channel_id=1, source_target_pairs={{0,32},{32,64},{64,96},{96,128},{128,160},{160,192},{192,224},{224... | collective-permute-start | bytes 1966088 | tf_op jit(solution)/shard_map/while/body/eval_jaxpr/ppermute | solution.py:13
  200.4 14.3 %collective-permute-start = (f32[320,512]{1,0:T(8,128)S(1)}, f32[320,512]{1,0:T(8,128)S(1)}, u32[]{:S(2)}, u32[]{:S(2)}) collective-permute-start(f32[320,512]{1,0:T(8,128)S(1)} %get-tuple-element.228), channel_id=1, source_target_pairs={{0,32},{32,64},{64,96},{96,128},{128,160},{160,192},{192,224},{224... | collective-permute-start | bytes 1966088 | tf_op jit(solution)/shard_map/while/body/eval_jaxpr/ppermute | solution.py:13
  215.1 14.3 %collective-permute-start = (f32[320,512]{1,0:T(8,128)S(1)}, f32[320,512]{1,0:T(8,128)S(1)}, u32[]{:S(2)}, u32[]{:S(2)}) collective-permute-start(f32[320,512]{1,0:T(8,128)S(1)} %get-tuple-element.228), channel_id=1, source_target_pairs={{0,32},{32,64},{64,96},{96,128},{128,160},{160,192},{192,224},{224... | collective-permute-start | bytes 1966088 | tf_op jit(solution)/shard_map/while/body/eval_jaxpr/ppermute | solution.py:13
  229.7 14.3 %collective-permute-start = (f32[320,512]{1,0:T(8,128)S(1)}, f32[320,512]{1,0:T(8,128)S(1)}, u32[]{:S(2)}, u32[]{:S(2)}) collective-permute-start(f32[320,512]{1,0:T(8,128)S(1)} %get-tuple-element.228), channel_id=1, source_target_pairs={{0,32},{32,64},{64,96},{96,128},{128,160},{160,192},{192,224},{224... | collective-permute-start | bytes 1966088 | tf_op jit(solution)/shard_map/while/body/eval_jaxpr/ppermute | solution.py:13
  244.4 14.3 %collective-permute-start = (f32[320,512]{1,0:T(8,128)S(1)}, f32[320,512]{1,0:T(8,128)S(1)}, u32[]{:S(2)}, u32[]{:S(2)}) collective-permute-start(f32[320,512]{1,0:T(8,128)S(1)} %get-tuple-element.228), channel_id=1, source_target_pairs={{0,32},{32,64},{64,96},{96,128},{128,160},{160,192},{192,224},{224... | collective-permute-start | bytes 1966088 | tf_op jit(solution)/shard_map/while/body/eval_jaxpr/ppermute | solution.py:13
  259.1 14.3 %collective-permute-start = (f32[320,512]{1,0:T(8,128)S(1)}, f32[320,512]{1,0:T(8,128)S(1)}, u32[]{:S(2)}, u32[]{:S(2)}) collective-permute-start(f32[320,512]{1,0:T(8,128)S(1)} %get-tuple-element.228), channel_id=1, source_target_pairs={{0,32},{32,64},{64,96},{96,128},{128,160},{160,192},{192,224},{224... | collective-permute-start | bytes 1966088 | tf_op jit(solution)/shard_map/while/body/eval_jaxpr/ppermute | solution.py:13
  273.7 14.3 %collective-permute-start = (f32[320,512]{1,0:T(8,128)S(1)}, f32[320,512]{1,0:T(8,128)S(1)}, u32[]{:S(2)}, u32[]{:S(2)}) collective-permute-start(f32[320,512]{1,0:T(8,128)S(1)} %get-tuple-element.228), channel_id=1, source_target_pairs={{0,32},{32,64},{64,96},{96,128},{128,160},{160,192},{192,224},{224... | collective-permute-start | bytes 1966088 | tf_op jit(solution)/shard_map/while/body/eval_jaxpr/ppermute | solution.py:13
  288.4 14.3 %collective-permute-start = (f32[320,512]{1,0:T(8,128)S(1)}, f32[320,512]{1,0:T(8,128)S(1)}, u32[]{:S(2)}, u32[]{:S(2)}) collective-permute-start(f32[320,512]{1,0:T(8,128)S(1)} %get-tuple-element.228), channel_id=1, source_target_pairs={{0,32},{32,64},{64,96},{96,128},{128,160},{160,192},{192,224},{224... | collective-permute-start | bytes 1966088 | tf_op jit(solution)/shard_map/while/body/eval_jaxpr/ppermute | solution.py:13
  303.1 14.3 %collective-permute-start = (f32[320,512]{1,0:T(8,128)S(1)}, f32[320,512]{1,0:T(8,128)S(1)}, u32[]{:S(2)}, u32[]{:S(2)}) collective-permute-start(f32[320,512]{1,0:T(8,128)S(1)} %get-tuple-element.228), channel_id=1, source_target_pairs={{0,32},{32,64},{64,96},{96,128},{128,160},{160,192},{192,224},{224... | collective-permute-start | bytes 1966088 | tf_op jit(solution)/shard_map/while/body/eval_jaxpr/ppermute | solution.py:13
  317.7 1.2 copy-start.4
Sparse Core Ops, SparseCore 0:
  11.3 79.4 all-gather.1
  319.1 150.8 reduce-scatter.1
where the time goes:
time: 479 us; the launch traced here: 478 us
  waiting for transfers between devices  286 us (60%)
  blocking collectives  120 us (25%)
  starting transfers between devices  29.1 us (6%)
  matrix products  18.6 us (4%)
  between operations  14.2 us (3%)
  other arithmetic  4.89 us (1%)
    ppermute x15, waiting for transfers between devices, passed_along(): lax.ppermute(shard, axis, [(i, (i + by) % devices) for i in range(devices)])  185 us
    psum x1, blocking collectives, local(): gain_total, bias_total = lax.psum((gain_term, bias_term), ('blk', 'dp'))  120 us
    all_gather x1, waiting for transfers between devices, local(): weight_piece = lax.all_gather(w_value, 'blk', axis=0, tiled=True)  76.8 us
    ppermute x15, starting transfers between devices, passed_along(): lax.ppermute(shard, axis, [(i, (i + by) % devices) for i in range(devices)])  29 us
    reduce_scatter x1, waiting for transfers between devices, local(): lax.psum_scatter(weight_block, 'dp', scatter_dimension=1, tiled=True)  23.1 us
  transfers between devices with their start and end apart: 17, of which 17 were waited for; matrix products, arithmetic and copies ran while one was open for 3% of the time, Pallas kernels for 0%

commit v1 on v0

v1 whole, which is shorter than its diff:
```python
import math

import jax
import jax.numpy as jnp
from jax import lax
from jax.experimental import pallas as pl
from jax.experimental.pallas import tpu as pltpu
from jax.sharding import PartitionSpec as P

MESH = pl.DeviceIdType.MESH
F32, BF16 = jnp.float32, jnp.bfloat16

D = 5120
HD = 128
ROWS = 128
GROUPS = 4
PER_GROUP = 5
KV = GROUPS * HD
QD = KV * PER_GROUP
NX, NY, NZ = 4, 4, 16
SHARE = 320
PAIR = 2 * SHARE
BLOCKS = D // PAIR
WIDE = 384
COLUMNS = 16
SMALL = PAIR + KV
N_DP = 32
COPIES = 95


def dot(a, b, dims):
    return lax.dot_general(a, b, (dims, ((), ())), preferred_element_type=F32)


def lane_tiles(a):
    total = a[:, :HD]
    for i in range(1, a.shape[1] // HD):
        total = total + a[:, i * HD : (i + 1) * HD]
    return total


def kernel(
    x_any, q_any, k_any, go_any, doc_ref, gain_ref, bias_ref, w_any,
    att_any, gi_any, gw_ref, gg_ref, gb_ref,
    xv, qv, kv, gov, hid, inv_ref, prob, vgb, vt, wf, xh, bias_term, value,
    hgrad, att, gi, pt, yr, zs, zr, small, sx, sy_own, sy, sz_own, sz, sg_own, sg,
    local_sem, send_sem, recv_sem,
):
    blk, dp = lax.axis_index("blk"), lax.axis_index("dp")
    x, yh, c = lax.div(blk, 4), lax.rem(lax.div(blk, 2), 2), lax.rem(blk, 2)
    z, yl = lax.div(dp, 2), lax.rem(dp, 2)
    y, half = yh * 2 + yl, lax.rem(z, 2)
    me = x * 2 + c

    def place(x, yh, c, z, yl):
        return (x * 4 + yh * 2 + c, z * 2 + yl)

    def on_y(y, c):
        return place(x, lax.div(y, 2), c, z, lax.rem(y, 2))

    def plus(a, by, n):
        return lax.rem(a + by, n)

    used = [0]

    def remote(src, dst, to):
        i = used[0]
        used[0] += 1
        return pltpu.make_async_remote_copy(
            src_ref=src,
            dst_ref=dst,
            send_sem=send_sem.at[i],
            recv_sem=recv_sem.at[i],
            device_id=to,
            device_id_type=MESH,
        )

    sent = []

    def send(src, dst, to):
        copy = remote(src, dst, to)
        copy.start()
        sent.append(copy)
        return copy

    loads = [
        pltpu.make_async_copy(w_any.at[pl.ds(0, 160)], wf.at[x, yh, c, 0], local_sem.at[0]),
        pltpu.make_async_copy(w_any.at[pl.ds(160, 160)], wf.at[x, yh, c, 1], local_sem.at[1]),
        pltpu.make_async_copy(x_any, xv, local_sem.at[2]),
        pltpu.make_async_copy(q_any, qv, local_sem.at[3]),
        pltpu.make_async_copy(k_any, kv, local_sem.at[4]),
        pltpu.make_async_copy(go_any, gov, local_sem.at[5]),
    ]
    for copy in loads:
        copy.start()

    near = [(dx, dc) for dx in (2, 1, 3, 0) for dc in (0, 1) if (dx, dc) != (0, 0)]
    sibling = place(x, yh, 1 - c, z, yl)
    across = place(x, 1 - yh, c, z, 1 - yl)

    barrier = pltpu.get_barrier_semaphore()
    partners = [place(plus(x, dx, NX), yh, plus(c, dc, 2), z, yl) for dx, dc in near]
    partners += [on_y(plus(y, dy, NY), plus(c, dc, 2)) for dy in (1, 2, 3) for dc in (0, 1)]
    partners += [place(x, yh, c, plus(z, dz, NZ), yl) for dz in range(1, NZ)]
    for partner in partners:
        pl.semaphore_signal(barrier, inc=1, device_id=partner, device_id_type=MESH)
    pl.semaphore_wait(barrier, len(partners))

    def block(k, y_hi, h):
        return wf.at[plus(x, NX - k, NX), y_hi, c, h]

    def pass_on(ref, to):
        return send(ref, ref, to)

    loads[0].wait()
    loads[1].wait()
    along_x, along_y, along_z, beside = {}, {}, {}, []
    for k in (2, 1, 3):
        along_x[k] = pass_on(block(0, yh, half), place(plus(x, k, NX), yh, c, z, yl))
    along_y[0] = pass_on(block(0, yh, half), across)
    beside.append(pass_on(block(0, yh, half), sibling))
    beside.append(pass_on(block(0, yh, 1 - half), sibling))

    loads[2].wait()

    def squares(j, total):
        part = xv[:, pl.ds(pl.multiple_of(j * PAIR, HD), PAIR)].astype(F32)
        return total + lane_tiles(part * part)

    total = lax.fori_loop(0, BLOCKS, squares, jnp.zeros((ROWS, HD), F32))
    inverse = lax.rsqrt(jnp.sum(total, axis=1, keepdims=True) * (1.0 / D) + 1e-06)
    inv_ref[...] = jnp.broadcast_to(inverse, (ROWS, HD))

    def normalise(j, carry):
        columns = pl.ds(pl.multiple_of(j * PAIR, HD), PAIR)
        normed = xv[:, columns].astype(F32) * inv_ref[:, :1]
        hid[j] = (normed * gain_ref[:, columns]).astype(BF16)
        return carry

    lax.fori_loop(0, BLOCKS, normalise, 0)

    hidden_sent = []
    for dx, dc in near:
        to_x, to_c = plus(x, dx, NX), plus(c, dc, 2)
        hidden_sent.append(send(hid.at[to_x * 2 + to_c], xh.at[me], place(to_x, yh, to_c, z, yl)))
    xh[me] = hid[me]

    up = place(x, yh, c, plus(z, 1, NZ), yl)
    down = place(x, yh, c, plus(z, NZ - 1, NZ), yl)

    def spread(k, y_hi, is_up, key):
        along_z[key] = pass_on(block(k, y_hi, half), up if is_up else down)
        beside.append(pass_on(block(k, y_hi, half), sibling))

    for k in (1, 3, 2):
        along_x[k].wait_recv()
        along_y[k] = pass_on(block(k, yh, half), across)
        spread(k, yh, k != 3, (0, k))

    for copy in loads[3:]:
        copy.wait()
    doc_row = jnp.broadcast_to(doc_ref[...].astype(F32), (ROWS, ROWS))
    positions = lax.broadcasted_iota(jnp.int32, (ROWS, ROWS), 0)
    key_positions = lax.broadcasted_iota(jnp.int32, (ROWS, ROWS), 1)
    allowed = (positions >= key_positions) & (doc_row == doc_row.T)

    def stacked(ref, g):
        heads = range(g * PER_GROUP, (g + 1) * PER_GROUP)
        return jnp.concatenate([ref[:, h * HD : (h + 1) * HD] for h in heads], axis=0)

    for g in range(GROUPS):
        group = slice(g * HD, (g + 1) * HD)
        scores = dot(stacked(qv, g), kv[:, group], ((1,), (1,))) * (1.0 / math.sqrt(HD))
        scores = jnp.where(allowed[None], scores.reshape(PER_GROUP, ROWS, ROWS), -1e30)
        exponent = jnp.exp(scores - jnp.max(scores, axis=-1, keepdims=True))
        chances = exponent / jnp.sum(exponent, axis=-1, keepdims=True)
        chances = chances.reshape(PER_GROUP * ROWS, ROWS).astype(BF16)
        prob[g] = chances
        value_grad = dot(chances, stacked(gov, g), ((0,), (0,)))
        bias_term[:, group] = jnp.sum(value_grad, axis=0, keepdims=True)
        vgb[:, group] = value_grad.astype(BF16)
        vt[group, pl.ds(pl.multiple_of(me * HD, HD), HD)] = value_grad.T.astype(BF16)

    def turned(x, c):
        return vt.at[:, pl.ds(pl.multiple_of((x * 2 + c) * HD, HD), HD)]

    turned_x = {}
    for k in (2, 1, 3):
        turned_x[k] = pass_on(turned(x, c), place(plus(x, k, NX), yh, c, z, yl))
    turned_beside = [pass_on(turned(x, c), sibling)]

    for k in (0, 1, 3, 2):
        along_y[k].wait_recv()
        spread(k, 1 - yh, k in (0, 3), (1, k))
    for k in (1, 3, 2):
        turned_x[k].wait_recv()
        turned_beside.append(pass_on(turned(plus(x, NX - k, NX), c), sibling))
    for (other, k), copy in along_z.items():
        copy.wait_recv()
        beside.append(pass_on(block(k, 1 - yh if other else yh, 1 - half), sibling))

    for copy in hidden_sent + turned_beside:
        copy.wait_recv()

    def product(i, carry):
        rows = pl.ds(pl.multiple_of(i * 128, 128), 128)
        part = dot(vt[rows, :], xh[...].reshape(8 * ROWS, PAIR), ((1,), (0,)))
        part = part.astype(BF16).reshape(4, 2, COLUMNS, PAIR)
        to = pl.ds(pl.multiple_of(i * 64, 64), 64)
        pt[0, to, :] = part[:, 0].reshape(64, PAIR)
        pt[1, to, :] = part[:, 1].reshape(64, PAIR)
        return carry

    lax.fori_loop(0, 4, product, 0)

    y_first = used[0]
    used[0] += 4
    crossing = []
    for side in (0, 1):
        for to_c in (0, 1):
            i = y_first + side * 2 + to_c
            to_y = 2 * c + side
            src, dst = pt.at[side, :, pl.ds(to_c * 256, WIDE)], yr.at[y]
            mine = (to_y == y) & (c == to_c)
            there = pltpu.make_async_remote_copy(
                src_ref=src,
                dst_ref=dst,
                send_sem=send_sem.at[i],
                recv_sem=recv_sem.at[y_first + y],
                device_id=on_y(to_y, to_c),
                device_id_type=MESH,
            )
            here = pltpu.make_async_copy(src, dst, recv_sem.at[y_first + y])
            crossing.append((mine, there))

            @pl.when(mine)
            def _():
                here.start()

            @pl.when(jnp.logical_not(mine))
            def _():
                there.start()

    for copy in beside:
        copy.wait_recv()

    value[...] = jnp.zeros_like(value)

    def with_block(j, row_sum):
        columns = pl.ds(pl.multiple_of(j * PAIR, HD), PAIR)
        weights = wf[lax.div(j, 2), lax.rem(j, 2)].reshape(PAIR, KV)
        value[...] += dot(hid[j], weights, ((1,), (0,)))
        back = dot(vgb[...], weights, ((1,), (1,))).astype(BF16)
        hgrad[j] = back
        wide = back.astype(F32) * (xv[:, columns].astype(F32) * inv_ref[:, :1])
        small[j, :, :PAIR] = jnp.sum(wide, axis=0, keepdims=True)
        small[j, :, PAIR:] = bias_term[...]
        return row_sum + lane_tiles(wide * gain_ref[:, columns])

    row_sum = lax.fori_loop(0, BLOCKS, with_block, jnp.zeros((ROWS, HD), F32))

    small_sent = []
    for dx, dc in near:
        to_x, to_c = plus(x, dx, NX), plus(c, dc, 2)
        small_sent.append(send(small.at[to_x * 2 + to_c], sx.at[me], place(to_x, yh, to_c, z, yl)))
    sx[me] = small[me]

    value_b = (value[...] + bias_ref[...]).astype(BF16)
    for g in range(GROUPS):
        mixed = dot(prob[g], value_b[:, g * HD : (g + 1) * HD], ((1,), (0,))).astype(BF16)
        for i in range(PER_GROUP):
            h = g * PER_GROUP + i
            att[:, h * HD : (h + 1) * HD] = mixed[i * ROWS : (i + 1) * ROWS]
    att_out = pltpu.make_async_copy(att, att_any, local_sem.at[6])
    att_out.start()

    for copy in small_sent:
        copy.wait_recv()
    sy_own[...] = jnp.sum(sx[...], axis=0)
    small_y = [send(sy_own, sy.at[y], on_y(plus(y, dy, NY), c)) for dy in (1, 2, 3)]
    sy[y] = sy_own[...]

    for i in range(NY):
        pltpu.make_async_copy(yr.at[i], yr.at[i], recv_sem.at[y_first + i]).wait()
    over_y = yr[0].astype(F32)
    for i in range(1, NY):
        over_y = over_y + yr[i].astype(F32)
    zs[...] = over_y.astype(BF16).reshape(NZ, COLUMNS, WIDE)
    columns_z = []
    for dz in range(1, NZ):
        to_z = plus(z, dz, NZ)
        columns_z.append(send(zs.at[to_z], zr.at[z], place(x, yh, c, to_z, yl)))
    zr[z] = zs[z]

    for copy in small_y:
        copy.wait_recv()
    sz_own[...] = jnp.sum(sy[...], axis=0)
    small_z = []
    for dz in range(1, NZ):
        small_z.append(send(sz_own, sz.at[z], place(x, yh, c, plus(z, dz, NZ), yl)))
    sz[z] = sz_own[...]

    mean = jnp.sum(row_sum, axis=1, keepdims=True) * (1.0 / D)

    def inputs_gradient(j, carry):
        columns = pl.ds(pl.multiple_of(j * PAIR, HD), PAIR)
        inverse = inv_ref[:, :1]
        normed = xv[:, columns].astype(F32) * inverse
        scaled = hgrad[j].astype(F32) * gain_ref[:, columns]
        gi[:, columns] = (inverse * (scaled - normed * mean)).astype(BF16)
        return carry

    lax.fori_loop(0, BLOCKS, inputs_gradient, 0)
    gi_out = pltpu.make_async_copy(gi, gi_any, local_sem.at[7])
    gi_out.start()

    for copy in small_z:
        copy.wait_recv()
    small_total = jnp.sum(sz[...], axis=0) * (1.0 / N_DP)
    sg_own[...] = small_total[:, :PAIR]
    gb_ref[...] = small_total[:, PAIR:]
    gathered = []
    for dx, dc in near:
        to = place(plus(x, dx, NX), yh, plus(c, dc, 2), z, yl)
        gathered.append(send(sg_own, sg.at[me], to))
    sg[me] = sg_own[...]

    for copy in columns_z:
        copy.wait_recv()
    over_z = zr[0].astype(F32)
    for i in range(1, NZ):
        over_z = over_z + zr[i].astype(F32)
    over_z = over_z * (1.0 / N_DP)
    gw_ref[...] = jnp.where(c == 0, over_z[:, :SHARE], over_z[:, WIDE - SHARE :])

    for copy in gathered:
        copy.wait_recv()
    gg_ref[...] = sg[...]

    for copy in sent:
        copy.wait_send()
    for mine, there in crossing:

        @pl.when(jnp.logical_not(mine))
        def _():
            there.wait_send()

    att_out.wait()
    gi_out.wait()


def local(inputs, queries, keys, doc_ids, grad_out, gain, bias, w_value):
    whole = pl.BlockSpec(memory_space=pltpu.VMEM)
    anywhere = pl.BlockSpec(memory_space=pl.ANY)
    attention, grad_inputs, grad_w, grad_gain, grad_bias = pl.pallas_call(
        kernel,
        out_shape=(
            jax.ShapeDtypeStruct((ROWS, QD), BF16),
            jax.ShapeDtypeStruct((ROWS, D), BF16),
            jax.ShapeDtypeStruct((COLUMNS, SHARE), F32),
            jax.ShapeDtypeStruct((BLOCKS, 1, PAIR), F32),
            jax.ShapeDtypeStruct((1, KV), F32),
        ),
        in_specs=[anywhere] * 4 + [whole] * 3 + [anywhere],
        out_specs=(anywhere, anywhere, whole, whole, whole),
        scratch_shapes=[
            pltpu.VMEM((ROWS, D), BF16),
            pltpu.VMEM((ROWS, QD), BF16),
            pltpu.VMEM((ROWS, KV), BF16),
            pltpu.VMEM((ROWS, QD), BF16),
            pltpu.VMEM((BLOCKS, ROWS, PAIR), BF16),
            pltpu.VMEM((ROWS, HD), F32),
            pltpu.VMEM((GROUPS, PER_GROUP * ROWS, ROWS), BF16),
            pltpu.VMEM((ROWS, KV), BF16),
            pltpu.VMEM((KV, 8 * ROWS), BF16),
            pltpu.VMEM((NX, 2, 2, 2, SHARE // 2, KV), BF16),
            pltpu.VMEM((8, ROWS, PAIR), BF16),
            pltpu.VMEM((1, KV), F32),
            pltpu.VMEM((ROWS, KV), F32),
            pltpu.VMEM((BLOCKS, ROWS, PAIR), BF16),
            pltpu.VMEM((ROWS, QD), BF16),
            pltpu.VMEM((ROWS, D), BF16),
            pltpu.VMEM((2, KV // 2, PAIR), BF16),
            pltpu.VMEM((NY, KV // 2, WIDE), BF16),
            pltpu.VMEM((NZ, COLUMNS, WIDE), BF16),
            pltpu.VMEM((NZ, COLUMNS, WIDE), BF16),
            pltpu.VMEM((BLOCKS, 1, SMALL), F32),
            pltpu.VMEM((8, 1, SMALL), F32),
            pltpu.VMEM((1, SMALL), F32),
            pltpu.VMEM((NY, 1, SMALL), F32),
            pltpu.VMEM((1, SMALL), F32),
            pltpu.VMEM((NZ, 1, SMALL), F32),
            pltpu.VMEM((1, PAIR), F32),
            pltpu.VMEM((8, 1, PAIR), F32),
            pltpu.SemaphoreType.DMA((8,)),
            pltpu.SemaphoreType.DMA((COPIES,)),
            pltpu.SemaphoreType.DMA((COPIES,)),
        ],
        compiler_params=pltpu.CompilerParams(
            collective_id=0, has_side_effects=True, vmem_limit_bytes=40 * 1024 * 1024
        ),
    )(
        inputs, queries, keys, grad_out, doc_ids.reshape(1, ROWS), gain.reshape(1, D),
        bias.reshape(1, KV), w_value,
    )
    return attention, grad_inputs, grad_w.T, grad_gain.reshape(D), grad_bias.reshape(KV)


def solution(mesh):
    placed = (
        P(("blk", "dp"), None),
        P(("blk", "dp"), None),
        P(("blk", "dp"), None),
        P(("blk", "dp")),
        P(("blk", "dp"), None),
        P(),
        P(),
        P("blk", None),
    )
    return jax.shard_map(
        local,
        mesh=mesh,
        in_specs=placed,
        out_specs=(P(("blk", "dp"), None), P(("blk", "dp"), None), P("blk", "dp"), P(), P()),
        check_vma=False,
    )
```

time: 479 us -> 90.5 us (0.19)
  the two profiles are of different devices: /device:TPU:6 before, /device:TPU:1 now
where the time goes in v1:
time: 90.5 us; the launch traced here: 90.1 us
  Pallas kernels  78.4 us (87%)
  local copies, waits for them, and re-layouts  11.1 us (12%)
    pallas_call x1, Pallas kernels, local(): pl.pallas_call(kernel, out_shape=(jax.ShapeDtypeStruct((ROWS, QD), BF16),...  78.4 us
    unnamed x21, local copies, waits for them, and re-layouts  11.1 us

profile of v1, /device:TPU:1, one launch (start us, length us, event | category | flops | bytes accessed | tf_op | source)
XLA Modules:
  0.0 90.1 jit_solution(3446205872175354037)
XLA Ops:
  0.6 0.0 copy-start
  0.6 1.3 %copy-done = bf16[128,5120]{1,0:T(8,128)(2,1)S(1)} copy-done((bf16[128,5120]{1,0:T(8,128)(2,1)S(1)}, bf16[128,5120]{1,0:T(8,128)(2,1)}, u32[]{:S(2)}) %copy-start) | copy-done | bytes 1310744
  2.0 0.0 copy-start.1
  2.0 1.1 %copy-done.1 = bf16[128,2560]{1,0:T(8,128)(2,1)S(1)} copy-done((bf16[128,2560]{1,0:T(8,128)(2,1)S(1)}, bf16[128,2560]{1,0:T(8,128)(2,1)}, u32[]{:S(2)}) %copy-start.1) | copy-done | bytes 655384
  3.0 0.0 copy-start.2
  3.0 1.1 %copy-done.2 = bf16[128,2560]{1,0:T(8,128)(2,1)S(1)} copy-done((bf16[128,2560]{1,0:T(8,128)(2,1)S(1)}, bf16[128,2560]{1,0:T(8,128)(2,1)}, u32[]{:S(2)}) %copy-start.2) | copy-done | bytes 655384
  4.1 0.0 copy-start.3
  4.1 1.0 %copy-done.3 = bf16[320,512]{1,0:T(8,128)(2,1)S(1)} copy-done((bf16[320,512]{1,0:T(8,128)(2,1)S(1)}, bf16[320,512]{1,0:T(8,128)(2,1)}, u32[]{:S(2)}) %copy-start.3) | copy-done | bytes 327704
  5.1 0.0 copy-start.4
  5.1 0.9 %copy-done.4 = bf16[128,512]{1,0:T(8,128)(2,1)S(1)} copy-done((bf16[128,512]{1,0:T(8,128)(2,1)S(1)}, bf16[128,512]{1,0:T(8,128)(2,1)}, u32[]{:S(2)}) %copy-start.4) | copy-done | bytes 131096
  6.0 0.0 copy-start.5
  6.0 0.7 copy-done.5
  6.7 0.0 copy-start.6
  6.7 0.7 copy-done.6
  7.4 0.0 copy-start.7
  7.4 0.7 copy-done.7
  8.1 78.4 %shard_map.119 = (bf16[128,2560]{1,0:T(8,128)(2,1)S(1)}, bf16[128,5120]{1,0:T(8,128)(2,1)S(1)}, f32[16,320]{1,0:T(8,128)S(1)}, f32[8,1,640]{2,1,0:T(1,128)S(1)}, f32[1,512]{1,0:T(1,128)S(1)}) custom-call(bf16[128,5120]{1,0:T(8,128)(2,1)S(1)} %copy-done, bf16[128,2560]{1,0:T(8,128)(2,1)S(1)} %copy-done.1, bf16[128,512]{1,0:T(8,128)(2,1)S(1)} %copy-done.4, ...), custom_call_target="tpu_custom_call" | custom-call | tf_op jit(solution)/shard_map/pallas_call | solution.py:355
  86.4 0.8 copy.18
  87.3 1.1 %copy.19 = bf16[128,5120]{1,0:T(8,128)(2,1)} copy(bf16[128,5120]{1,0:T(8,128)(2,1)S(1)} %get-tuple-element.21) | data formatting | bytes 2621440
  88.3 0.6 copy.20
  88.9 0.6 copy.21
  89.6 0.6 copy.22
Async XLA Ops:
  0.6 1.3 %copy-start = (bf16[128,5120]{1,0:T(8,128)(2,1)S(1)}, bf16[128,5120]{1,0:T(8,128)(2,1)}, u32[]{:S(2)}) copy-start(bf16[128,5120]{1,0:T(8,128)(2,1)} %x_any.1) | copy-start | bytes 3932164
  2.0 1.1 %copy-start.1 = (bf16[128,2560]{1,0:T(8,128)(2,1)S(1)}, bf16[128,2560]{1,0:T(8,128)(2,1)}, u32[]{:S(2)}) copy-start(bf16[128,2560]{1,0:T(8,128)(2,1)} %q_any.1) | copy-start | bytes 1966084
  3.0 1.1 %copy-start.2 = (bf16[128,2560]{1,0:T(8,128)(2,1)S(1)}, bf16[128,2560]{1,0:T(8,128)(2,1)}, u32[]{:S(2)}) copy-start(bf16[128,2560]{1,0:T(8,128)(2,1)} %go_any.1) | copy-start | bytes 1966084
  4.1 1.0 %copy-start.3 = (bf16[320,512]{1,0:T(8,128)(2,1)S(1)}, bf16[320,512]{1,0:T(8,128)(2,1)}, u32[]{:S(2)}) copy-start(bf16[320,512]{1,0:T(8,128)(2,1)} %w_any.1) | copy-start | bytes 983044
  5.1 0.9 %copy-start.4 = (bf16[128,512]{1,0:T(8,128)(2,1)S(1)}, bf16[128,512]{1,0:T(8,128)(2,1)}, u32[]{:S(2)}) copy-start(bf16[128,512]{1,0:T(8,128)(2,1)} %k_any.1) | copy-start | bytes 393220
  6.0 0.7 copy-start.5
  6.7 0.7 copy-start.6
  7.4 0.7 copy-start.7

commit v2 on v1

v2 whole, which is shorter than its diff:
```python
import math

import jax
import jax.numpy as jnp
from jax import lax
from jax.experimental import pallas as pl
from jax.experimental.pallas import tpu as pltpu
from jax.sharding import PartitionSpec as P

MESH = pl.DeviceIdType.MESH
F32, BF16 = jnp.float32, jnp.bfloat16

D = 5120
HD = 128
ROWS = 128
GROUPS = 4
PER_GROUP = 5
KV = GROUPS * HD
QD = KV * PER_GROUP
NX, NY, NZ = 4, 4, 16
SHARE = 320
QUARTER = SHARE // 4
PAIR = 2 * SHARE
BLOCKS = D // PAIR
WIDE = 384
COLUMNS = 16
SMALL = PAIR + KV
N_DP = 32
COPIES = 120
PIECES = 4


def dot(a, b, dims):
    return lax.dot_general(a, b, (dims, ((), ())), preferred_element_type=F32)


def lane_tiles(a):
    total = a[:, :HD]
    for i in range(1, a.shape[1] // HD):
        total = total + a[:, i * HD : (i + 1) * HD]
    return total


def kernel(
    x_any, q_any, k_any, go_any, doc_ref, gain_ref, bias_ref, w_any,
    att_any, gi_any, gw_ref, gg_ref, gb_ref,
    xv, qv, kv, gov, hid, inv_ref, prob, vgb, vt, wf, xh, value,
    hgrad, att, gi, pt, yr, zs, zr, sy_own, sy, sz_own, sz, sg_own, sg,
    local_sem, send_sem, recv_sem, lower_sem, upper_sem,
):
    blk, dp = lax.axis_index("blk"), lax.axis_index("dp")
    x, yh, c = lax.div(blk, 4), lax.rem(lax.div(blk, 2), 2), lax.rem(blk, 2)
    z, yl = lax.div(dp, 2), lax.rem(dp, 2)
    y, half = yh * 2 + yl, lax.rem(z, 2)
    me = x * 2 + c

    def place(x, yh, c, z, yl):
        return (x * 4 + yh * 2 + c, z * 2 + yl)

    def on_y(y, c):
        return place(x, lax.div(y, 2), c, z, lax.rem(y, 2))

    def plus(a, by, n):
        return lax.rem(a + by, n)

    used = [0]

    def take(n):
        used[0] += n
        return used[0] - n

    def remote(src, dst, to, sent_at, received_at):
        return pltpu.make_async_remote_copy(
            src_ref=src,
            dst_ref=dst,
            send_sem=send_sem.at[sent_at],
            recv_sem=recv_sem.at[received_at],
            device_id=to,
            device_id_type=MESH,
        )

    sent = []

    def send(src, dst, to):
        i = take(1)
        copy = remote(src, dst, to, i, i)
        copy.start()
        sent.append(copy)
        return copy

    def pass_on(ref, to):
        return send(ref, ref, to)

    loads = [
        pltpu.make_async_copy(x_any, xv, local_sem.at[0]),
        pltpu.make_async_copy(q_any, qv, local_sem.at[1]),
        pltpu.make_async_copy(k_any, kv, local_sem.at[2]),
        pltpu.make_async_copy(go_any, gov, local_sem.at[3]),
    ]
    loads += [
        pltpu.make_async_copy(
            w_any.at[pl.ds(i * QUARTER, QUARTER)], wf.at[x, yh, c, i], local_sem.at[4 + i]
        )
        for i in range(4)
    ]
    for copy in loads:
        copy.start()

    near = [(dx, dc) for dx in (2, 1, 3, 0) for dc in (0, 1) if (dx, dc) != (0, 0)]
    sibling = place(x, yh, 1 - c, z, yl)
    up = place(x, yh, c, plus(z, 1, NZ), yl)
    down = place(x, yh, c, plus(z, NZ - 1, NZ), yl)

    barrier = pltpu.get_barrier_semaphore()
    partners = [place(plus(x, dx, NX), yh, plus(c, dc, 2), z, yl) for dx, dc in near]
    partners += [on_y(plus(y, dy, NY), plus(c, dc, 2)) for dy in (1, 2, 3) for dc in (0, 1)]
    partners += [up, down]
    for partner in partners:
        pl.semaphore_signal(barrier, inc=1, device_id=partner, device_id_type=MESH)

    loads[0].wait()

    def squares(j, total):
        part = xv[:, pl.ds(pl.multiple_of(j * PAIR, HD), PAIR)].astype(F32)
        return total + lane_tiles(part * part)

    total = lax.fori_loop(0, BLOCKS, squares, jnp.zeros((ROWS, HD), F32))
    inverse = lax.rsqrt(jnp.sum(total, axis=1, keepdims=True) * (1.0 / D) + 1e-06)
    inv_ref[...] = jnp.broadcast_to(inverse, (ROWS, HD))

    pl.semaphore_wait(barrier, len(partners))

    rounds = [0]

    def relay():
        if rounds[0] > 0:
            pl.semaphore_wait(lower_sem, 1)
            pl.semaphore_wait(upper_sem, 1)
        if rounds[0] < NZ // 2 - 1:
            pl.semaphore_signal(lower_sem, inc=1, device_id=up, device_id_type=MESH)
            pl.semaphore_signal(upper_sem, inc=1, device_id=down, device_id_type=MESH)
        rounds[0] += 1

    relay()

    def quarter(k, y_hi, y_lo):
        return wf.at[plus(x, NX - k, NX), y_hi, c, half * 2 + y_lo]

    def half_block(k, y_hi, h):
        return wf.at[plus(x, NX - k, NX), y_hi, c, pl.ds(h * 2, 2)]

    for copy in loads[4:]:
        copy.wait()
    along_x, along_y, along_z, beside = {}, {}, {}, {}

    others = (
        place(x, yh, c, z, 1 - yl),
        place(x, 1 - yh, c, z, yl),
        place(x, 1 - yh, c, z, 1 - yl),
    )

    def spread_y(k):
        for i in range(1 if k == 0 else 0, 3):
            along_y[k, i] = pass_on(quarter(k, yh, yl), others[i])

    def spread_z(k, other, is_up):
        y_hi = 1 - yh if other else yh
        along_z[other, k] = pass_on(half_block(k, y_hi, half), up if is_up else down)
        beside[other, k, 0] = pass_on(half_block(k, y_hi, half), sibling)

    def spread_beside(k, other):
        along_z[other, k].wait_recv()
        y_hi = 1 - yh if other else yh
        beside[other, k, 1] = pass_on(half_block(k, y_hi, 1 - half), sibling)

    spread_y(0)
    beside[0, 0, 0] = pass_on(half_block(0, yh, 0), sibling)
    beside[0, 0, 1] = pass_on(half_block(0, yh, 1), sibling)
    for k in (2, 1, 3):
        along_x[k] = pass_on(quarter(0, yh, yl), place(plus(x, k, NX), yh, c, z, yl))

    def normalise(j, carry):
        columns = pl.ds(pl.multiple_of(j * PAIR, HD), PAIR)
        normed = xv[:, columns].astype(F32) * inv_ref[:, :1]
        hid[j] = (normed * gain_ref[:, columns]).astype(BF16)
        return carry

    lax.fori_loop(0, BLOCKS, normalise, 0)

    def send_hidden(first, width):
        columns = pl.ds(first, width)
        copies = []
        for dx, dc in near:
            to_x, to_c = plus(x, dx, NX), plus(c, dc, 2)
            src, dst = hid.at[to_x * 2 + to_c, :, columns], xh.at[me, :, columns]
            copies.append(send(src, dst, place(to_x, yh, to_c, z, yl)))
        return copies

    hidden_a = send_hidden(0, WIDE)
    xh[me] = hid[me]

    for copy in loads[1:4]:
        copy.wait()
    doc_row = jnp.broadcast_to(doc_ref[...].astype(F32), (ROWS, ROWS))
    positions = lax.broadcasted_iota(jnp.int32, (ROWS, ROWS), 0)
    key_positions = lax.broadcasted_iota(jnp.int32, (ROWS, ROWS), 1)
    allowed = (positions >= key_positions) & (doc_row == doc_row.T)

    def stacked(ref, g):
        heads = range(g * PER_GROUP, (g + 1) * PER_GROUP)
        return jnp.concatenate([ref[:, h * HD : (h + 1) * HD] for h in heads], axis=0)

    for g in range(GROUPS):
        group = slice(g * HD, (g + 1) * HD)
        scores = dot(stacked(qv, g), kv[:, group], ((1,), (1,))) * (1.0 / math.sqrt(HD))
        scores = jnp.where(allowed[None], scores.reshape(PER_GROUP, ROWS, ROWS), -1e30)
        exponent = jnp.exp(scores - jnp.max(scores, axis=-1, keepdims=True))
        chances = exponent / jnp.sum(exponent, axis=-1, keepdims=True)
        chances = chances.reshape(PER_GROUP * ROWS, ROWS).astype(BF16)
        prob[g] = chances
        value_grad = dot(chances, stacked(gov, g), ((0,), (0,)))
        vgb[:, group] = value_grad.astype(BF16)
        vt[group, pl.ds(pl.multiple_of(me * HD, HD), HD)] = value_grad.T.astype(BF16)

    def turned(x, c):
        return vt.at[:, pl.ds(pl.multiple_of((x * 2 + c) * HD, HD), HD)]

    turned_x = {}
    for k in (2, 1, 3):
        turned_x[k] = pass_on(turned(x, c), place(plus(x, k, NX), yh, c, z, yl))
    turned_beside = [pass_on(turned(x, c), sibling)]
    hidden_b = send_hidden(WIDE, PAIR - WIDE)
    relay()

    for i in (1, 2):
        along_y[0, i].wait_recv()
    spread_z(0, 1, True)
    relay()
    for k in (1, 3, 2):
        along_x[k].wait_recv()
        spread_y(k)
    relay()
    spread_beside(0, 1)
    relay()
    for k in (1, 3, 2):
        for i in range(3):
            along_y[k, i].wait_recv()
        spread_z(k, 0, k != 3)
        spread_z(k, 1, k == 3)
    relay()

    for k in (1, 3, 2):
        turned_x[k].wait_recv()
        turned_beside.append(pass_on(turned(plus(x, NX - k, NX), c), sibling))
    relay()

    def product(first, width):
        def step(i, carry):
            rows = pl.ds(pl.multiple_of(i * 128, 128), 128)
            columns = slice(first, first + width)
            part = dot(vt[rows, :], xh[:, :, columns].reshape(8 * ROWS, width), ((1,), (0,)))
            part = part.astype(BF16).reshape(4, 2, COLUMNS, width)
            to = pl.ds(pl.multiple_of(i * 64, 64), 64)
            pt[0, to, columns] = part[:, 0].reshape(64, width)
            pt[1, to, columns] = part[:, 1].reshape(64, width)
            return carry

        lax.fori_loop(0, 4, step, 0)

    y_sent, y_received = take(4), used[0] - 4
    crossing = []

    def send_y(to_c):
        for side in (0, 1):
            to_y = 2 * c + side
            src, dst = pt.at[side, :, pl.ds(to_c * 256, WIDE)], yr.at[y]
            mine = (to_y == y) & (c == to_c)
            there = remote(src, dst, on_y(to_y, to_c), y_sent + side * 2 + to_c, y_received + y)
            here = pltpu.make_async_copy(src, dst, recv_sem.at[y_received + y])
            crossing.append((mine, there))

            @pl.when(mine)
            def _():
                here.start()

            @pl.when(jnp.logical_not(mine))
            def _():
                there.start()

    z_first = take(NZ - 1)
    columns_z = []
    for dz in range(1, NZ):
        to_z = plus(z, dz, NZ)
        i = z_first + dz - 1
        columns_z.append(remote(zs.at[to_z], zr.at[z], place(x, yh, c, to_z, yl), i, i))

    def sum_y():
        for i in range(NY):
            pltpu.make_async_copy(yr.at[i], yr.at[i], recv_sem.at[y_received + i]).wait()
        over_y = yr[0].astype(F32)
        for i in range(1, NY):
            over_y = over_y + yr[i].astype(F32)
        zs[...] = over_y.astype(BF16).reshape(NZ, COLUMNS, WIDE)
        for copy in columns_z:
            copy.start()
        zr[z] = zs[z]

    for copy in hidden_a + turned_beside:
        copy.wait_recv()
    product(0, WIDE)
    send_y(0)
    relay()
    pl.when(c == 0)(sum_y)

    for copy in hidden_b:
        copy.wait_recv()
    product(WIDE, PAIR - WIDE)
    send_y(1)

    for key in ((0, 0, 0), (0, 0, 1), (1, 0, 0), (1, 0, 1)):
        beside.pop(key).wait_recv()
    ones = jnp.ones((8, 8 * ROWS), BF16)
    sy_own[:, PAIR:] = dot(ones, vt[...], ((1,), (1,)))[:1]

    def weighted(i, total):
        columns = pl.ds(pl.multiple_of(i * 128, 128), 128)
        turned_w = wf[x, c, :, :, :, columns].reshape(PAIR, 128).astype(F32).T
        turned_w = turned_w.reshape(4, 2, COLUMNS, PAIR)
        rows = pl.ds(pl.multiple_of(i * 64, 64), 64)
        for side in (0, 1):
            both = pt[side, rows, :].astype(F32) * turned_w[:, side].reshape(64, PAIR)
            total = total + jnp.sum(both, axis=0, keepdims=True)
        return total

    gain_sum = lax.fori_loop(0, 4, weighted, jnp.zeros((1, PAIR), F32))
    sy_own[:, :PAIR] = gain_sum / gain_ref[:, pl.ds(pl.multiple_of(me * PAIR, HD), PAIR)]
    small_y = [send(sy_own, sy.at[y], on_y(plus(y, dy, NY), c)) for dy in (1, 2, 3)]
    sy[y] = sy_own[...]

    for k in (1, 3, 2):
        spread_beside(k, 0)
        spread_beside(k, 1)

    def with_block(i, row_sum):
        from_x, from_y = plus(x, NX - lax.div(i, 2), NX), plus(yh, lax.rem(i, 2), 2)
        j = from_x * 2 + from_y
        columns = pl.ds(pl.multiple_of(j * PAIR, HD), PAIR)
        weights = wf[from_x, from_y].reshape(PAIR, KV)
        value[...] += dot(hid[j], weights, ((1,), (0,)))
        back = dot(vgb[...], weights, ((1,), (1,))).astype(BF16)
        hgrad[j] = back
        wide = back.astype(F32) * (xv[:, columns].astype(F32) * inv_ref[:, :1])
        return row_sum + lane_tiles(wide * gain_ref[:, columns])

    value[...] = jnp.zeros_like(value)
    row_sum = lax.fori_loop(0, 2, with_block, jnp.zeros((ROWS, HD), F32))

    for copy in small_y:
        copy.wait_recv()
    sz_own[...] = jnp.sum(sy[...], axis=0)
    small_z = []
    for dz in range(1, NZ):
        small_z.append(send(sz_own, sz.at[z], place(x, yh, c, plus(z, dz, NZ), yl)))
    sz[z] = sz_own[...]

    pl.when(c == 1)(sum_y)

    for copy in beside.values():
        copy.wait_recv()
    row_sum = lax.fori_loop(2, BLOCKS, with_block, row_sum)

    value_b = (value[...] + bias_ref[...]).astype(BF16)
    for g in range(GROUPS):
        mixed = dot(prob[g], value_b[:, g * HD : (g + 1) * HD], ((1,), (0,))).astype(BF16)
        for i in range(PER_GROUP):
            h = g * PER_GROUP + i
            att[:, h * HD : (h + 1) * HD] = mixed[i * ROWS : (i + 1) * ROWS]
    att_out = pltpu.make_async_copy(att, att_any, local_sem.at[8])
    att_out.start()

    mean = jnp.sum(row_sum, axis=1, keepdims=True) * (1.0 / D)

    def inputs_gradient(j, carry):
        columns = pl.ds(pl.multiple_of(j * PAIR, HD), PAIR)
        inverse = inv_ref[:, :1]
        normed = xv[:, columns].astype(F32) * inverse
        scaled = hgrad[j].astype(F32) * gain_ref[:, columns]
        gi[:, columns] = (inverse * (scaled - normed * mean)).astype(BF16)
        return carry

    lax.fori_loop(0, BLOCKS, inputs_gradient, 0)
    gi_out = pltpu.make_async_copy(gi, gi_any, local_sem.at[9])
    gi_out.start()

    for copy in small_z:
        copy.wait_recv()
    small_total = jnp.sum(sz[...], axis=0) * (1.0 / N_DP)
    sg_own[...] = small_total[:, :PAIR]
    gb_ref[...] = small_total[:, PAIR:]
    gathered = []
    for dx, dc in near:
        to = place(plus(x, dx, NX), yh, plus(c, dc, 2), z, yl)
        gathered.append(send(sg_own, sg.at[me], to))
    sg[me] = sg_own[...]

    for copy in columns_z:
        copy.wait_recv()
    over_z = zr[0].astype(F32)
    for i in range(1, NZ):
        over_z = over_z + zr[i].astype(F32)
    over_z = over_z * (1.0 / N_DP)
    gw_ref[...] = jnp.where(c == 0, over_z[:, :SHARE], over_z[:, WIDE - SHARE :])

    for copy in gathered:
        copy.wait_recv()
    gg_ref[...] = sg[...]

    for copy in sent + columns_z:
        copy.wait_send()
    for mine, there in crossing:

        @pl.when(jnp.logical_not(mine))
        def _():
            there.wait_send()

    att_out.wait()
    gi_out.wait()


def hand_over(
    att_in, gi_in, gw_in, gg_in, gb_in, att_out, gi_out, gw_out, gg_out, gb_out, att, gi, sem
):
    copies = []
    for i in range(PIECES):
        rows = pl.ds(i * (ROWS // PIECES), ROWS // PIECES)
        for source, held, out in ((gi_in, gi, gi_out), (att_in, att, att_out)):
            a, b = sem.at[0, len(copies)], sem.at[1, len(copies)]
            into = pltpu.make_async_copy(source.at[rows], held.at[rows], a)
            into.start()
            copies.append((into, pltpu.make_async_copy(held.at[rows], out.at[rows], b)))
    gw_out[...] = gw_in[...]
    gg_out[...] = gg_in[...]
    gb_out[...] = gb_in[...]
    for into, out in copies:
        into.wait()
        out.start()
    for into, out in copies:
        out.wait()


def local(inputs, queries, keys, doc_ids, grad_out, gain, bias, w_value):
    whole = pl.BlockSpec(memory_space=pltpu.VMEM)
    anywhere = pl.BlockSpec(memory_space=pl.ANY)
    summed = pl.pallas_call(
        kernel,
        out_shape=(
            jax.ShapeDtypeStruct((ROWS, QD), BF16),
            jax.ShapeDtypeStruct((ROWS, D), BF16),
            jax.ShapeDtypeStruct((COLUMNS, SHARE), F32),
            jax.ShapeDtypeStruct((BLOCKS, 1, PAIR), F32),
            jax.ShapeDtypeStruct((1, KV), F32),
        ),
        in_specs=[anywhere] * 4 + [whole] * 3 + [anywhere],
        out_specs=(anywhere, anywhere, whole, whole, whole),
        scratch_shapes=[
            pltpu.VMEM((ROWS, D), BF16),
            pltpu.VMEM((ROWS, QD), BF16),
            pltpu.VMEM((ROWS, KV), BF16),
            pltpu.VMEM((ROWS, QD), BF16),
            pltpu.VMEM((BLOCKS, ROWS, PAIR), BF16),
            pltpu.VMEM((ROWS, HD), F32),
            pltpu.VMEM((GROUPS, PER_GROUP * ROWS, ROWS), BF16),
            pltpu.VMEM((ROWS, KV), BF16),
            pltpu.VMEM((KV, 8 * ROWS), BF16),
            pltpu.VMEM((NX, 2, 2, 4, QUARTER, KV), BF16),
            pltpu.VMEM((8, ROWS, PAIR), BF16),
            pltpu.VMEM((ROWS, KV), F32),
            pltpu.VMEM((BLOCKS, ROWS, PAIR), BF16),
            pltpu.VMEM((ROWS, QD), BF16),
            pltpu.VMEM((ROWS, D), BF16),
            pltpu.VMEM((2, KV // 2, PAIR), BF16),
            pltpu.VMEM((NY, KV // 2, WIDE), BF16),
            pltpu.VMEM((NZ, COLUMNS, WIDE), BF16),
            pltpu.VMEM((NZ, COLUMNS, WIDE), BF16),
            pltpu.VMEM((1, SMALL), F32),
            pltpu.VMEM((NY, 1, SMALL), F32),
            pltpu.VMEM((1, SMALL), F32),
            pltpu.VMEM((NZ, 1, SMALL), F32),
            pltpu.VMEM((1, PAIR), F32),
            pltpu.VMEM((8, 1, PAIR), F32),
            pltpu.SemaphoreType.DMA((10,)),
            pltpu.SemaphoreType.DMA((COPIES,)),
            pltpu.SemaphoreType.DMA((COPIES,)),
            pltpu.SemaphoreType.REGULAR,
            pltpu.SemaphoreType.REGULAR,
        ],
        compiler_params=pltpu.CompilerParams(
            collective_id=0, has_side_effects=True, vmem_limit_bytes=60 * 1024 * 1024
        ),
    )(
        inputs, queries, keys, grad_out, doc_ids.reshape(1, ROWS), gain.reshape(1, D),
        bias.reshape(1, KV), w_value,
    )
    attention, grad_inputs, grad_w, grad_gain, grad_bias = pl.pallas_call(
        hand_over,
        out_shape=(
            jax.ShapeDtypeStruct((ROWS, QD), BF16),
            jax.ShapeDtypeStruct((ROWS, D), BF16),
            jax.ShapeDtypeStruct((COLUMNS, SHARE), F32),
            jax.ShapeDtypeStruct((BLOCKS, 1, PAIR), F32),
            jax.ShapeDtypeStruct((1, KV), F32),
        ),
        in_specs=[anywhere, anywhere, whole, whole, whole],
        out_specs=(anywhere, anywhere, whole, whole, whole),
        scratch_shapes=[
            pltpu.VMEM((ROWS, QD), BF16),
            pltpu.VMEM((ROWS, D), BF16),
            pltpu.SemaphoreType.DMA((2, 2 * PIECES)),
        ],
        compiler_params=pltpu.CompilerParams(vmem_limit_bytes=60 * 1024 * 1024),
    )(*summed)
    return attention, grad_inputs, grad_w.T, grad_gain.reshape(D), grad_bias.reshape(KV)


def solution(mesh):
    placed = (
        P(("blk", "dp"), None),
        P(("blk", "dp"), None),
        P(("blk", "dp"), None),
        P(("blk", "dp")),
        P(("blk", "dp"), None),
        P(),
        P(),
        P("blk", None),
    )
    return jax.shard_map(
        local,
        mesh=mesh,
        in_specs=placed,
        out_specs=(P(("blk", "dp"), None), P(("blk", "dp"), None), P("blk", "dp"), P(), P()),
        check_vma=False,
    )
```

time: 90.5 us -> 76.5 us (0.85)
  local copies, waits for them, and re-layouts: 11.1 us -> 0 us
  Pallas kernels: 78.4 us -> 75.5 us
    unnamed x21 -> x0, local copies, waits for them, and re-layouts: 11.1 us -> none
    pallas_call x1, Pallas kernels: 78.4 us -> 71.8 us  [local(): pl.pallas_call(kernel, out_shape=(jax.ShapeDtypeStruct((ROWS, QD), BF16),...]
    pallas_call x0 -> x1, Pallas kernels: none -> 3.76 us  [local(): pl.pallas_call(hand_over, out_shape=(jax.ShapeDtypeStruct((ROWS, QD), BF1...]
where the time goes in v2:
time: 76.5 us; the launch traced here: 76.2 us
  Pallas kernels  75.5 us (99%)
    pallas_call x1, Pallas kernels, local(): pl.pallas_call(kernel, out_shape=(jax.ShapeDtypeStruct((ROWS, QD), BF16),...  71.8 us
    pallas_call x1, Pallas kernels, local(): pl.pallas_call(hand_over, out_shape=(jax.ShapeDtypeStruct((ROWS, QD), BF1...  3.76 us

profile of v2, /device:TPU:1, one launch (start us, length us, event | category | flops | bytes accessed | tf_op | source)
XLA Modules:
  0.0 76.2 jit_solution(13316888400086934709)
XLA Ops:
  0.6 71.8 %shard_map.119 = (bf16[128,2560]{1,0:T(8,128)(2,1)}, bf16[128,5120]{1,0:T(8,128)(2,1)}, f32[16,320]{1,0:T(8,128)}, f32[8,1,640]{2,1,0:T(1,128)}, f32[1,512]{1,0:T(1,128)}) custom-call(bf16[128,5120]{1,0:T(8,128)(2,1)} %x_any.1, bf16[128,2560]{1,0:T(8,128)(2,1)} %q_any.1, bf16[128,512]{1,0:T(8,128)(2,1)} %k_any.1, bf16[128,2560]{1,0:T(8,128)(2,1)} %go_any.1, ...), custom_call_target="tpu_custom_call" | custom-call | tf_op jit(solution)/shard_map/pallas_call | solution.py:454
  72.4 3.8 %shard_map.120 = (bf16[128,2560]{1,0:T(8,128)(2,1)}, bf16[128,5120]{1,0:T(8,128)(2,1)}, f32[16,320]{1,0:T(8,128)}, f32[8,1,640]{2,1,0:T(1,128)}, f32[1,512]{1,0:T(1,128)}) custom-call(bf16[128,2560]{1,0:T(8,128)(2,1)} %get-tuple-element.15.att_in, bf16[128,5120]{1,0:T(8,128)(2,1)} %get-tuple-element.16.gi_in, f32[16,320]{1,0:T(8,128)} %get-tuple-element.17.gw_in, ...), custom_call_target="tpu_custom_call" | custom-call | tf_op jit(solution)/shard_map/pallas_call | solution.py:504

commit v3 on v2

--- a/solution.py
+++ b/solution.py
@@ -27,7 +27,7 @@
 SMALL = PAIR + KV
 N_DP = 32
 COPIES = 120
-PIECES = 4
+FAR_FIRST = (8, 7, 9, 6, 10, 5, 11, 4, 12, 3, 13, 2, 14, 1, 15)
 
 
 def dot(a, b, dims):
@@ -42,10 +42,10 @@
 
 
 def kernel(
-    x_any, q_any, k_any, go_any, doc_ref, gain_ref, bias_ref, w_any,
-    att_any, gi_any, gw_ref, gg_ref, gb_ref,
-    xv, qv, kv, gov, hid, inv_ref, prob, vgb, vt, wf, xh, value,
-    hgrad, att, gi, pt, yr, zs, zr, sy_own, sy, sz_own, sz, sg_own, sg,
+    x_any, q_any, k_any, go_any, doc_any, gain_any, bias_any, w_any,
+    att, gi, gw_ref, gg_ref, gb_ref,
+    xv, qv, kv, gov, doc_ref, gain_ref, bias_ref, hid, inv_ref, prob, vgb, vt, wf, xh, value,
+    hgrad, pt, yr, zs, zr, sy_own, sy, sz_own, sz, sg_own, sg,
     local_sem, send_sem, recv_sem, lower_sem, upper_sem,
 ):
     blk, dp = lax.axis_index("blk"), lax.axis_index("dp")
@@ -96,6 +96,9 @@
         pltpu.make_async_copy(q_any, qv, local_sem.at[1]),
         pltpu.make_async_copy(k_any, kv, local_sem.at[2]),
         pltpu.make_async_copy(go_any, gov, local_sem.at[3]),
+        pltpu.make_async_copy(doc_any, doc_ref, local_sem.at[8]),
+        pltpu.make_async_copy(bias_any, bias_ref, local_sem.at[9]),
+        pltpu.make_async_copy(gain_any, gain_ref, local_sem.at[10]),
     ]
     loads += [
         pltpu.make_async_copy(
@@ -118,16 +121,6 @@
     for partner in partners:
         pl.semaphore_signal(barrier, inc=1, device_id=partner, device_id_type=MESH)
 
-    loads[0].wait()
-
-    def squares(j, total):
-        part = xv[:, pl.ds(pl.multiple_of(j * PAIR, HD), PAIR)].astype(F32)
-        return total + lane_tiles(part * part)
-
-    total = lax.fori_loop(0, BLOCKS, squares, jnp.zeros((ROWS, HD), F32))
-    inverse = lax.rsqrt(jnp.sum(total, axis=1, keepdims=True) * (1.0 / D) + 1e-06)
-    inv_ref[...] = jnp.broadcast_to(inverse, (ROWS, HD))
-
     pl.semaphore_wait(barrier, len(partners))
 
     rounds = [0]
@@ -149,7 +142,7 @@
     def half_block(k, y_hi, h):
         return wf.at[plus(x, NX - k, NX), y_hi, c, pl.ds(h * 2, 2)]
 
-    for copy in loads[4:]:
+    for copy in loads[7:]:
         copy.wait()
     along_x, along_y, along_z, beside = {}, {}, {}, {}
 
@@ -178,6 +171,17 @@
     beside[0, 0, 1] = pass_on(half_block(0, yh, 1), sibling)
     for k in (2, 1, 3):
         along_x[k] = pass_on(quarter(0, yh, yl), place(plus(x, k, NX), yh, c, z, yl))
+
+    loads[0].wait()
+    loads[6].wait()
+
+    def squares(j, total):
+        part = xv[:, pl.ds(pl.multiple_of(j * PAIR, HD), PAIR)].astype(F32)
+        return total + lane_tiles(part * part)
+
+    total = lax.fori_loop(0, BLOCKS, squares, jnp.zeros((ROWS, HD), F32))
+    inverse = lax.rsqrt(jnp.sum(total, axis=1, keepdims=True) * (1.0 / D) + 1e-06)
+    inv_ref[...] = jnp.broadcast_to(inverse, (ROWS, HD))
 
     def normalise(j, carry):
         columns = pl.ds(pl.multiple_of(j * PAIR, HD), PAIR)
@@ -199,7 +203,7 @@
     hidden_a = send_hidden(0, WIDE)
     xh[me] = hid[me]
 
-    for copy in loads[1:4]:
+    for copy in loads[1:6]:
         copy.wait()
     doc_row = jnp.broadcast_to(doc_ref[...].astype(F32), (ROWS, ROWS))
     positions = lax.broadcasted_iota(jnp.int32, (ROWS, ROWS), 0)
@@ -229,7 +233,6 @@
     for k in (2, 1, 3):
         turned_x[k] = pass_on(turned(x, c), place(plus(x, k, NX), yh, c, z, yl))
     turned_beside = [pass_on(turned(x, c), sibling)]
-    hidden_b = send_hidden(WIDE, PAIR - WIDE)
     relay()
 
     for i in (1, 2):
@@ -242,6 +245,9 @@
     relay()
     spread_beside(0, 1)
     relay()
+    for copy in hidden_a:
+        copy.wait_recv()
+    hidden_b = send_hidden(WIDE, PAIR - WIDE)
     for k in (1, 3, 2):
         for i in range(3):
             along_y[k, i].wait_recv()
@@ -289,7 +295,7 @@
 
     z_first = take(NZ - 1)
     columns_z = []
-    for dz in range(1, NZ):
+    for dz in FAR_FIRST:
         to_z = plus(z, dz, NZ)
         i = z_first + dz - 1
         columns_z.append(remote(zs.at[to_z], zr.at[z], place(x, yh, c, to_z, yl), i, i))
@@ -305,13 +311,11 @@
             copy.start()
         zr[z] = zs[z]
 
-    for copy in hidden_a + turned_beside:
+    for copy in turned_beside:
         copy.wait_recv()
     product(0, WIDE)
     send_y(0)
     relay()
-    pl.when(c == 0)(sum_y)
-
     for copy in hidden_b:
         copy.wait_recv()
     product(WIDE, PAIR - WIDE)
@@ -336,6 +340,7 @@
     sy_own[:, :PAIR] = gain_sum / gain_ref[:, pl.ds(pl.multiple_of(me * PAIR, HD), PAIR)]
     small_y = [send(sy_own, sy.at[y], on_y(plus(y, dy, NY), c)) for dy in (1, 2, 3)]
     sy[y] = sy_own[...]
+    pl.when(c == 0)(sum_y)
 
     for k in (1, 3, 2):
         spread_beside(k, 0)
@@ -359,7 +364,7 @@
         copy.wait_recv()
     sz_own[...] = jnp.sum(sy[...], axis=0)
     small_z = []
-    for dz in range(1, NZ):
+    for dz in FAR_FIRST:
         small_z.append(send(sz_own, sz.at[z], place(x, yh, c, plus(z, dz, NZ), yl)))
     sz[z] = sz_own[...]
 
@@ -375,8 +380,6 @@
         for i in range(PER_GROUP):
             h = g * PER_GROUP + i
             att[:, h * HD : (h + 1) * HD] = mixed[i * ROWS : (i + 1) * ROWS]
-    att_out = pltpu.make_async_copy(att, att_any, local_sem.at[8])
-    att_out.start()
 
     mean = jnp.sum(row_sum, axis=1, keepdims=True) * (1.0 / D)
 
@@ -389,8 +392,6 @@
         return carry
 
     lax.fori_loop(0, BLOCKS, inputs_gradient, 0)
-    gi_out = pltpu.make_async_copy(gi, gi_any, local_sem.at[9])
-    gi_out.start()
 
     for copy in small_z:
         copy.wait_recv()
@@ -423,50 +424,42 @@
         def _():
             there.wait_send()
 
-    att_out.wait()
-    gi_out.wait()
-
-
-def hand_over(
-    att_in, gi_in, gw_in, gg_in, gb_in, att_out, gi_out, gw_out, gg_out, gb_out, att, gi, sem
-):
-    copies = []
-    for i in range(PIECES):
-        rows = pl.ds(i * (ROWS // PIECES), ROWS // PIECES)
-        for source, held, out in ((gi_in, gi, gi_out), (att_in, att, att_out)):
-            a, b = sem.at[0, len(copies)], sem.at[1, len(copies)]
-            into = pltpu.make_async_copy(source.at[rows], held.at[rows], a)
-            into.start()
-            copies.append((into, pltpu.make_async_copy(held.at[rows], out.at[rows], b)))
-    gw_out[...] = gw_in[...]
-    gg_out[...] = gg_in[...]
-    gb_out[...] = gb_in[...]
-    for into, out in copies:
-        into.wait()
-        out.start()
-    for into, out in copies:
-        out.wait()
+
+def hand_over(*refs):
+    results, outs, sem = refs[:5], refs[5:10], refs[10]
+    copies = [pltpu.make_async_copy(results[i], outs[i], sem.at[i]) for i in range(5)]
+    for copy in copies:
+        copy.start()
+    for copy in copies:
+        copy.wait()
 
 
 def local(inputs, queries, keys, doc_ids, grad_out, gain, bias, w_value):
     whole = pl.BlockSpec(memory_space=pltpu.VMEM)
     anywhere = pl.BlockSpec(memory_space=pl.ANY)
+    arguments = (
+        inputs, queries, keys, grad_out, doc_ids.reshape(1, ROWS), gain.reshape(1, D),
+        bias.reshape(1, KV), w_value,
+    )
     summed = pl.pallas_call(
         kernel,
         out_shape=(
-            jax.ShapeDtypeStruct((ROWS, QD), BF16),
-            jax.ShapeDtypeStruct((ROWS, D), BF16),
-            jax.ShapeDtypeStruct((COLUMNS, SHARE), F32),
-            jax.ShapeDtypeStruct((BLOCKS, 1, PAIR), F32),
-            jax.ShapeDtypeStruct((1, KV), F32),
+            pltpu.VMEM((ROWS, QD), BF16),
+            pltpu.VMEM((ROWS, D), BF16),
+            pltpu.VMEM((COLUMNS, SHARE), F32),
+            pltpu.VMEM((BLOCKS, 1, PAIR), F32),
+            pltpu.VMEM((1, KV), F32),
         ),
-        in_specs=[anywhere] * 4 + [whole] * 3 + [anywhere],
-        out_specs=(anywhere, anywhere, whole, whole, whole),
+        in_specs=[anywhere] * len(arguments),
+        out_specs=(whole,) * 5,
         scratch_shapes=[
             pltpu.VMEM((ROWS, D), BF16),
             pltpu.VMEM((ROWS, QD), BF16),
             pltpu.VMEM((ROWS, KV), BF16),
             pltpu.VMEM((ROWS, QD), BF16),
+            pltpu.VMEM((1, ROWS), jnp.int32),
+            pltpu.VMEM((1, D), F32),
+            pltpu.VMEM((1, KV), F32),
             pltpu.VMEM((BLOCKS, ROWS, PAIR), BF16),
             pltpu.VMEM((ROWS, HD), F32),
             pltpu.VMEM((GROUPS, PER_GROUP * ROWS, ROWS), BF16),
@@ -476,8 +469,6 @@
             pltpu.VMEM((8, ROWS, PAIR), BF16),
             pltpu.VMEM((ROWS, KV), F32),
             pltpu.VMEM((BLOCKS, ROWS, PAIR), BF16),
-            pltpu.VMEM((ROWS, QD), BF16),
-            pltpu.VMEM((ROWS, D), BF16),
             pltpu.VMEM((2, KV // 2, PAIR), BF16),
             pltpu.VMEM((NY, KV // 2, WIDE), BF16),
             pltpu.VMEM((NZ, COLUMNS, WIDE), BF16),
@@ -488,18 +479,17 @@
             pltpu.VMEM((NZ, 1, SMALL), F32),
             pltpu.VMEM((1, PAIR), F32),
             pltpu.VMEM((8, 1, PAIR), F32),
-            pltpu.SemaphoreType.DMA((10,)),
+            pltpu.SemaphoreType.DMA((11,)),
             pltpu.SemaphoreType.DMA((COPIES,)),
             pltpu.SemaphoreType.DMA((COPIES,)),
             pltpu.SemaphoreType.REGULAR,
             pltpu.SemaphoreType.REGULAR,
         ],
         compiler_params=pltpu.CompilerParams(
-            collective_id=0, has_side_effects=True, vmem_limit_bytes=60 * 1024 * 1024
+            collective_id=0, has_side_effects=True, vmem_limit_bytes=32 * 1024 * 1024
         ),
     )(
-        inputs, queries, keys, grad_out, doc_ids.reshape(1, ROWS), gain.reshape(1, D),
-        bias.reshape(1, KV), w_value,
+        *(pltpu.with_memory_space_constraint(argument, pltpu.HBM) for argument in arguments)
     )
     attention, grad_inputs, grad_w, grad_gain, grad_bias = pl.pallas_call(
         hand_over,
@@ -510,14 +500,10 @@
             jax.ShapeDtypeStruct((BLOCKS, 1, PAIR), F32),
             jax.ShapeDtypeStruct((1, KV), F32),
         ),
-        in_specs=[anywhere, anywhere, whole, whole, whole],
-        out_specs=(anywhere, anywhere, whole, whole, whole),
-        scratch_shapes=[
-            pltpu.VMEM((ROWS, QD), BF16),
-            pltpu.VMEM((ROWS, D), BF16),
-            pltpu.SemaphoreType.DMA((2, 2 * PIECES)),
-        ],
-        compiler_params=pltpu.CompilerParams(vmem_limit_bytes=60 * 1024 * 1024),
+        in_specs=[whole] * 5,
+        out_specs=(anywhere,) * 5,
+        scratch_shapes=[pltpu.SemaphoreType.DMA((5,))],
+        compiler_params=pltpu.CompilerParams(vmem_limit_bytes=16 * 1024 * 1024),
     )(*summed)
     return attention, grad_inputs, grad_w.T, grad_gain.reshape(D), grad_bias.reshape(KV)
 

time: 76.5 us -> 66 us (0.86)
  Pallas kernels: 75.5 us -> 65.2 us
    pallas_call x1, Pallas kernels: 71.8 us -> 63.9 us  [local(): pl.pallas_call(kernel, out_shape=(pltpu.VMEM((ROWS, QD), BF16), pltpu.VME...]
    pallas_call x1, Pallas kernels: 3.76 us -> 1.32 us  [local(): pl.pallas_call(hand_over, out_shape=(jax.ShapeDtypeStruct((ROWS, QD), BF1...]
where the time goes in v3:
time: 66 us; the launch traced here: 65.8 us
  Pallas kernels  65.2 us (99%)
    pallas_call x1, Pallas kernels, local(): pl.pallas_call(kernel, out_shape=(pltpu.VMEM((ROWS, QD), BF16), pltpu.VME...  63.9 us
    pallas_call x1, Pallas kernels, local(): pl.pallas_call(hand_over, out_shape=(jax.ShapeDtypeStruct((ROWS, QD), BF1...  1.32 us

profile of v3, /device:TPU:1, one launch (start us, length us, event | category | flops | bytes accessed | tf_op | source)
XLA Modules:
  0.0 65.8 jit_solution(15375334065420672817)
XLA Ops:
  0.6 63.9 %shard_map.119 = (bf16[128,2560]{1,0:T(8,128)(2,1)S(1)}, bf16[128,5120]{1,0:T(8,128)(2,1)S(1)}, f32[16,320]{1,0:T(8,128)S(1)}, f32[8,1,640]{2,1,0:T(1,128)S(1)}, f32[1,512]{1,0:T(1,128)S(1)}) custom-call(bf16[128,5120]{1,0:T(8,128)(2,1)} %x_any.1, bf16[128,2560]{1,0:T(8,128)(2,1)} %q_any.1, bf16[128,512]{1,0:T(8,128)(2,1)} %k_any.1, ...), custom_call_target="tpu_custom_call" | custom-call | tf_op jit(solution)/shard_map/pallas_call | solution.py:444
  64.5 1.3 %shard_map.120 = (bf16[128,2560]{1,0:T(8,128)(2,1)}, bf16[128,5120]{1,0:T(8,128)(2,1)}, f32[16,320]{1,0:T(8,128)}, f32[8,1,640]{2,1,0:T(1,128)}, f32[1,512]{1,0:T(1,128)}) custom-call(bf16[128,2560]{1,0:T(8,128)(2,1)S(1)} %get-tuple-element.15.refs_0_, bf16[128,5120]{1,0:T(8,128)(2,1)S(1)} %get-tuple-element.16.refs_1_, ...), custom_call_target="tpu_custom_call" | custom-call | tf_op jit(solution)/shard_map/pallas_call | solution.py:494

commit v4 on v3

--- a/solution.py
+++ b/solution.py
@@ -24,9 +24,9 @@
 BLOCKS = D // PAIR
 WIDE = 384
 COLUMNS = 16
-SMALL = PAIR + KV
+SMALL = PAIR + HD
 N_DP = 32
-COPIES = 120
+COPIES = 144
 FAR_FIRST = (8, 7, 9, 6, 10, 5, 11, 4, 12, 3, 13, 2, 14, 1, 15)
 
 
@@ -45,7 +45,7 @@
     x_any, q_any, k_any, go_any, doc_any, gain_any, bias_any, w_any,
     att, gi, gw_ref, gg_ref, gb_ref,
     xv, qv, kv, gov, doc_ref, gain_ref, bias_ref, hid, inv_ref, prob, vgb, vt, wf, xh, value,
-    hgrad, pt, yr, zs, zr, sy_own, sy, sz_own, sz, sg_own, sg,
+    hgrad, pt, yr, zs, zr, middle_own, middle_in, sz_own, sz, sg_own, sg,
     local_sem, send_sem, recv_sem, lower_sem, upper_sem,
 ):
     blk, dp = lax.axis_index("blk"), lax.axis_index("dp")
@@ -262,24 +262,26 @@
 
     def product(first, width):
         def step(i, carry):
-            rows = pl.ds(pl.multiple_of(i * 128, 128), 128)
+            rows = pl.ds(pl.multiple_of(i * 256, 256), 256)
             columns = slice(first, first + width)
             part = dot(vt[rows, :], xh[:, :, columns].reshape(8 * ROWS, width), ((1,), (0,)))
-            part = part.astype(BF16).reshape(4, 2, COLUMNS, width)
-            to = pl.ds(pl.multiple_of(i * 64, 64), 64)
-            pt[0, to, columns] = part[:, 0].reshape(64, width)
-            pt[1, to, columns] = part[:, 1].reshape(64, width)
+            part = part.astype(BF16).reshape(8, 2, COLUMNS, width)
+            to = pl.ds(pl.multiple_of(i * 128, 128), 128)
+            pt[0, to, columns] = part[:, 0].reshape(128, width)
+            pt[1, to, columns] = part[:, 1].reshape(128, width)
             return carry
 
-        lax.fori_loop(0, 4, step, 0)
-
+        lax.fori_loop(0, 2, step, 0)
+
+    parts = ((0, WIDE), (WIDE, PAIR - WIDE))
     y_sent, y_received = take(4), used[0] - 4
     crossing = []
 
     def send_y(to_c):
+        first, width = parts[to_c]
         for side in (0, 1):
             to_y = 2 * c + side
-            src, dst = pt.at[side, :, pl.ds(to_c * 256, WIDE)], yr.at[y]
+            src, dst = pt.at[side, :, pl.ds(first, width)], yr.at[y, :, pl.ds(0, width)]
             mine = (to_y == y) & (c == to_c)
             there = remote(src, dst, on_y(to_y, to_c), y_sent + side * 2 + to_c, y_received + y)
             here = pltpu.make_async_copy(src, dst, recv_sem.at[y_received + y])
@@ -294,53 +296,84 @@
                 there.start()
 
     z_first = take(NZ - 1)
-    columns_z = []
-    for dz in FAR_FIRST:
-        to_z = plus(z, dz, NZ)
-        i = z_first + dz - 1
-        columns_z.append(remote(zs.at[to_z], zr.at[z], place(x, yh, c, to_z, yl), i, i))
-
-    def sum_y():
+
+    def along_z_copies(width):
+        copies = []
+        for dz in FAR_FIRST:
+            to_z = plus(z, dz, NZ)
+            i = z_first + dz - 1
+            src, dst = zs.at[to_z, :, pl.ds(0, width)], zr.at[z, :, pl.ds(0, width)]
+            copies.append(remote(src, dst, place(x, yh, c, to_z, yl), i, i))
+        return copies
+
+    def sum_y(core):
+        width = parts[core][1]
         for i in range(NY):
-            pltpu.make_async_copy(yr.at[i], yr.at[i], recv_sem.at[y_received + i]).wait()
-        over_y = yr[0].astype(F32)
+            arrived = yr.at[i, :, pl.ds(0, width)]
+            pltpu.make_async_copy(arrived, arrived, recv_sem.at[y_received + i]).wait()
+        over_y = yr[0, :, :width].astype(F32)
         for i in range(1, NY):
-            over_y = over_y + yr[i].astype(F32)
-        zs[...] = over_y.astype(BF16).reshape(NZ, COLUMNS, WIDE)
-        for copy in columns_z:
+            over_y = over_y + yr[i, :, :width].astype(F32)
+        zs[:, :, :width] = over_y.astype(BF16).reshape(NZ, COLUMNS, width)
+        for copy in along_z_copies(width):
             copy.start()
-        zr[z] = zs[z]
+        zr[z, :, :width] = zs[z, :, :width]
+
+    def sum_z(core):
+        width = parts[core][1]
+        for copy in along_z_copies(width):
+            copy.wait()
+        over_z = zr[0, :, :width].astype(F32)
+        for i in range(1, NZ):
+            over_z = over_z + zr[i, :, :width].astype(F32)
+        return over_z * (1.0 / N_DP)
+
+    middle = take(1)
+
+    def middle_copy():
+        return remote(middle_own, middle_in, sibling, middle, middle)
 
     for copy in turned_beside:
         copy.wait_recv()
     product(0, WIDE)
     send_y(0)
     relay()
+
+    for key in ((0, 0, 0), (0, 0, 1), (1, 0, 0), (1, 0, 1)):
+        beside.pop(key).wait_recv()
+    ones = jnp.ones((8, 8 * ROWS), BF16)
+    one_head = pl.ds(pl.multiple_of(x * HD, HD), HD)
+    sz_own[:, PAIR:] = dot(ones, vt[one_head, :], ((1,), (1,)))[:1]
+
+    def weighted(first, width):
+        lanes = slice(first, first + width)
+
+        def step(i, total):
+            columns = pl.ds(pl.multiple_of(i * 128, 128), 128)
+            turned_w = wf[x, c, :, :, :, columns].reshape(PAIR, 128)[lanes].astype(F32).T
+            turned_w = turned_w.reshape(4, 2, COLUMNS, width)
+            rows = pl.ds(pl.multiple_of(i * 64, 64), 64)
+            for side in (0, 1):
+                both = pt[side, rows, lanes].astype(F32) * turned_w[:, side].reshape(64, width)
+                total = total + jnp.sum(both, axis=0, keepdims=True)
+            return total
+
+        total = lax.fori_loop(0, 4, step, jnp.zeros((1, width), F32))
+        own = pl.ds(pl.multiple_of(me * PAIR + first, HD), width)
+        sz_own[:, lanes] = total / gain_ref[:, own]
+
+    weighted(0, WIDE)
+
     for copy in hidden_b:
         copy.wait_recv()
     product(WIDE, PAIR - WIDE)
     send_y(1)
-
-    for key in ((0, 0, 0), (0, 0, 1), (1, 0, 0), (1, 0, 1)):
-        beside.pop(key).wait_recv()
-    ones = jnp.ones((8, 8 * ROWS), BF16)
-    sy_own[:, PAIR:] = dot(ones, vt[...], ((1,), (1,)))[:1]
-
-    def weighted(i, total):
-        columns = pl.ds(pl.multiple_of(i * 128, 128), 128)
-        turned_w = wf[x, c, :, :, :, columns].reshape(PAIR, 128).astype(F32).T
-        turned_w = turned_w.reshape(4, 2, COLUMNS, PAIR)
-        rows = pl.ds(pl.multiple_of(i * 64, 64), 64)
-        for side in (0, 1):
-            both = pt[side, rows, :].astype(F32) * turned_w[:, side].reshape(64, PAIR)
-            total = total + jnp.sum(both, axis=0, keepdims=True)
-        return total
-
-    gain_sum = lax.fori_loop(0, 4, weighted, jnp.zeros((1, PAIR), F32))
-    sy_own[:, :PAIR] = gain_sum / gain_ref[:, pl.ds(pl.multiple_of(me * PAIR, HD), PAIR)]
-    small_y = [send(sy_own, sy.at[y], on_y(plus(y, dy, NY), c)) for dy in (1, 2, 3)]
-    sy[y] = sy_own[...]
-    pl.when(c == 0)(sum_y)
+    weighted(WIDE, PAIR - WIDE)
+    small_z = []
+    for dz in FAR_FIRST:
+        small_z.append(send(sz_own, sz.at[z], place(x, yh, c, plus(z, dz, NZ), yl)))
+    sz[z] = sz_own[...]
+    pl.when(c == 0)(lambda: sum_y(0))
 
     for k in (1, 3, 2):
         spread_beside(k, 0)
@@ -360,19 +393,25 @@
     value[...] = jnp.zeros_like(value)
     row_sum = lax.fori_loop(0, 2, with_block, jnp.zeros((ROWS, HD), F32))
 
-    for copy in small_y:
-        copy.wait_recv()
-    sz_own[...] = jnp.sum(sy[...], axis=0)
-    small_z = []
-    for dz in FAR_FIRST:
-        small_z.append(send(sz_own, sz.at[z], place(x, yh, c, plus(z, dz, NZ), yl)))
-    sz[z] = sz_own[...]
-
-    pl.when(c == 1)(sum_y)
+    pl.when(c == 1)(lambda: sum_y(1))
 
     for copy in beside.values():
         copy.wait_recv()
     row_sum = lax.fori_loop(2, BLOCKS, with_block, row_sum)
+
+    for copy in small_z:
+        copy.wait_recv()
+    sg_own[...] = jnp.sum(sz[...], axis=0) * (1.0 / N_DP)
+    gathered = []
+    for dy in (2, 1, 3, 0):
+        for dx, dc in near + [(0, 0)]:
+            if (dx, dy, dc) != (0, 0, 0):
+                to_y = plus(y, dy, NY)
+                to = place(
+                    plus(x, dx, NX), lax.div(to_y, 2), plus(c, dc, 2), z, lax.rem(to_y, 2)
+                )
+                gathered.append(send(sg_own, sg.at[y * 8 + me], to))
+    sg[y * 8 + me] = sg_own[...]
 
     value_b = (value[...] + bias_ref[...]).astype(BF16)
     for g in range(GROUPS):
@@ -393,31 +432,34 @@
 
     lax.fori_loop(0, BLOCKS, inputs_gradient, 0)
 
-    for copy in small_z:
-        copy.wait_recv()
-    small_total = jnp.sum(sz[...], axis=0) * (1.0 / N_DP)
-    sg_own[...] = small_total[:, :PAIR]
-    gb_ref[...] = small_total[:, PAIR:]
-    gathered = []
-    for dx, dc in near:
-        to = place(plus(x, dx, NX), yh, plus(c, dc, 2), z, yl)
-        gathered.append(send(sg_own, sg.at[me], to))
-    sg[me] = sg_own[...]
-
-    for copy in columns_z:
-        copy.wait_recv()
-    over_z = zr[0].astype(F32)
-    for i in range(1, NZ):
-        over_z = over_z + zr[i].astype(F32)
-    over_z = over_z * (1.0 / N_DP)
-    gw_ref[...] = jnp.where(c == 0, over_z[:, :SHARE], over_z[:, WIDE - SHARE :])
+    @pl.when(c == 0)
+    def _():
+        over_z = sum_z(0)
+        gw_ref[...] = over_z[:, :SHARE]
+        middle_own[...] = over_z[:, WIDE - HD :]
+        middle_copy().start()
+
+
+    @pl.when(c == 1)
+    def _():
+        over_z = sum_z(1)
+        middle_copy().wait_recv()
+        gw_ref[...] = jnp.concatenate([middle_in[:, HD // 2 :], over_z], axis=1)
 
     for copy in gathered:
         copy.wait_recv()
-    gg_ref[...] = sg[...]
-
-    for copy in sent + columns_z:
+    over_all = jnp.sum(sg[...].reshape(NY, 8, 1, SMALL), axis=0)
+    gg_ref[...] = over_all[:, :, :PAIR]
+    for i in range(NX):
+        gb_ref[:, i * HD : (i + 1) * HD] = over_all[2 * i, :, PAIR:]
+
+    for copy in sent:
         copy.wait_send()
+
+    @pl.when(c == 0)
+    def _():
+        middle_copy().wait_send()
+
     for mine, there in crossing:
 
         @pl.when(jnp.logical_not(mine))
@@ -473,12 +515,12 @@
             pltpu.VMEM((NY, KV // 2, WIDE), BF16),
             pltpu.VMEM((NZ, COLUMNS, WIDE), BF16),
             pltpu.VMEM((NZ, COLUMNS, WIDE), BF16),
-            pltpu.VMEM((1, SMALL), F32),
-            pltpu.VMEM((NY, 1, SMALL), F32),
+            pltpu.VMEM((COLUMNS, HD), F32),
+            pltpu.VMEM((COLUMNS, HD), F32),
             pltpu.VMEM((1, SMALL), F32),
             pltpu.VMEM((NZ, 1, SMALL), F32),
-            pltpu.VMEM((1, PAIR), F32),
-            pltpu.VMEM((8, 1, PAIR), F32),
+            pltpu.VMEM((1, SMALL), F32),
+            pltpu.VMEM((8 * NY, 1, SMALL), F32),
             pltpu.SemaphoreType.DMA((11,)),
             pltpu.SemaphoreType.DMA((COPIES,)),
             pltpu.SemaphoreType.DMA((COPIES,)),

time: 66 us -> 62.2 us (0.942)
  Pallas kernels: 65.2 us -> 61.4 us
    pallas_call x1, Pallas kernels: 63.9 us -> 60.1 us  [local(): pl.pallas_call(kernel, out_shape=(pltpu.VMEM((ROWS, QD), BF16), pltpu.VME...]
where the time goes in v4:
time: 62.2 us; the launch traced here: 62.1 us
  Pallas kernels  61.4 us (99%)
  between operations  0.64 us (1%)
    pallas_call x1, Pallas kernels, local(): pl.pallas_call(kernel, out_shape=(pltpu.VMEM((ROWS, QD), BF16), pltpu.VME...  60.1 us
    pallas_call x1, Pallas kernels, local(): pl.pallas_call(hand_over, out_shape=(jax.ShapeDtypeStruct((ROWS, QD), BF1...  1.32 us

profile of v4, /device:TPU:1, one launch (start us, length us, event | category | flops | bytes accessed | tf_op | source)
XLA Modules:
  0.0 62.1 jit_solution(4016463598697376721)
XLA Ops:
  0.6 60.1 %shard_map.119 = (bf16[128,2560]{1,0:T(8,128)(2,1)S(1)}, bf16[128,5120]{1,0:T(8,128)(2,1)S(1)}, f32[16,320]{1,0:T(8,128)S(1)}, f32[8,1,640]{2,1,0:T(1,128)S(1)}, f32[1,512]{1,0:T(1,128)S(1)}) custom-call(bf16[128,5120]{1,0:T(8,128)(2,1)} %x_any.1, bf16[128,2560]{1,0:T(8,128)(2,1)} %q_any.1, bf16[128,512]{1,0:T(8,128)(2,1)} %k_any.1, ...), custom_call_target="tpu_custom_call" | custom-call | tf_op jit(solution)/shard_map/pallas_call | solution.py:486
  60.8 1.3 %shard_map.120 = (bf16[128,2560]{1,0:T(8,128)(2,1)}, bf16[128,5120]{1,0:T(8,128)(2,1)}, f32[16,320]{1,0:T(8,128)}, f32[8,1,640]{2,1,0:T(1,128)}, f32[1,512]{1,0:T(1,128)}) custom-call(bf16[128,2560]{1,0:T(8,128)(2,1)S(1)} %get-tuple-element.15.refs_0_, bf16[128,5120]{1,0:T(8,128)(2,1)S(1)} %get-tuple-element.16.refs_1_, ...), custom_call_target="tpu_custom_call" | custom-call | tf_op jit(solution)/shard_map/pallas_call | solution.py:536

commit v5 on v4

--- a/solution.py
+++ b/solution.py
@@ -109,7 +109,7 @@
     for copy in loads:
         copy.start()
 
-    near = [(dx, dc) for dx in (2, 1, 3, 0) for dc in (0, 1) if (dx, dc) != (0, 0)]
+    near = [(dx, dc) for dx in (1, 3, 2, 0) for dc in (0, 1) if (dx, dc) != (0, 0)]
     sibling = place(x, yh, 1 - c, z, yl)
     up = place(x, yh, c, plus(z, 1, NZ), yl)
     down = place(x, yh, c, plus(z, NZ - 1, NZ), yl)
@@ -398,6 +398,13 @@
     for copy in beside.values():
         copy.wait_recv()
     row_sum = lax.fori_loop(2, BLOCKS, with_block, row_sum)
+
+    value_b = (value[...] + bias_ref[...]).astype(BF16)
+    for g in range(GROUPS):
+        mixed = dot(prob[g], value_b[:, g * HD : (g + 1) * HD], ((1,), (0,))).astype(BF16)
+        for i in range(PER_GROUP):
+            h = g * PER_GROUP + i
+            att[:, h * HD : (h + 1) * HD] = mixed[i * ROWS : (i + 1) * ROWS]
 
     for copy in small_z:
         copy.wait_recv()
@@ -412,13 +419,6 @@
                 )
                 gathered.append(send(sg_own, sg.at[y * 8 + me], to))
     sg[y * 8 + me] = sg_own[...]
-
-    value_b = (value[...] + bias_ref[...]).astype(BF16)
-    for g in range(GROUPS):
-        mixed = dot(prob[g], value_b[:, g * HD : (g + 1) * HD], ((1,), (0,))).astype(BF16)
-        for i in range(PER_GROUP):
-            h = g * PER_GROUP + i
-            att[:, h * HD : (h + 1) * HD] = mixed[i * ROWS : (i + 1) * ROWS]
 
     mean = jnp.sum(row_sum, axis=1, keepdims=True) * (1.0 / D)
 

time: 62.2 us -> 60.2 us (0.968)
  Pallas kernels: 61.4 us -> 59.4 us
    pallas_call x1, Pallas kernels: 60.1 us -> 58.1 us  [local(): pl.pallas_call(kernel, out_shape=(pltpu.VMEM((ROWS, QD), BF16), pltpu.VME...]
where the time goes in v5:
time: 60.2 us; the launch traced here: 60.1 us
  Pallas kernels  59.4 us (99%)
  between operations  0.64 us (1%)
    pallas_call x1, Pallas kernels, local(): pl.pallas_call(kernel, out_shape=(pltpu.VMEM((ROWS, QD), BF16), pltpu.VME...  58.1 us
    pallas_call x1, Pallas kernels, local(): pl.pallas_call(hand_over, out_shape=(jax.ShapeDtypeStruct((ROWS, QD), BF1...  1.32 us

profile of v5, /device:TPU:1, one launch (start us, length us, event | category | flops | bytes accessed | tf_op | source)
XLA Modules:
  0.0 60.1 jit_solution(12599821578354196217)
XLA Ops:
  0.6 58.1 %shard_map.119 = (bf16[128,2560]{1,0:T(8,128)(2,1)S(1)}, bf16[128,5120]{1,0:T(8,128)(2,1)S(1)}, f32[16,320]{1,0:T(8,128)S(1)}, f32[8,1,640]{2,1,0:T(1,128)S(1)}, f32[1,512]{1,0:T(1,128)S(1)}) custom-call(bf16[128,5120]{1,0:T(8,128)(2,1)} %x_any.1, bf16[128,2560]{1,0:T(8,128)(2,1)} %q_any.1, bf16[128,512]{1,0:T(8,128)(2,1)} %k_any.1, ...), custom_call_target="tpu_custom_call" | custom-call | tf_op jit(solution)/shard_map/pallas_call | solution.py:486
  58.8 1.3 %shard_map.120 = (bf16[128,2560]{1,0:T(8,128)(2,1)}, bf16[128,5120]{1,0:T(8,128)(2,1)}, f32[16,320]{1,0:T(8,128)}, f32[8,1,640]{2,1,0:T(1,128)}, f32[1,512]{1,0:T(1,128)}) custom-call(bf16[128,2560]{1,0:T(8,128)(2,1)S(1)} %get-tuple-element.15.refs_0_, bf16[128,5120]{1,0:T(8,128)(2,1)S(1)} %get-tuple-element.16.refs_1_, ...), custom_call_target="tpu_custom_call" | custom-call | tf_op jit(solution)/shard_map/pallas_call | solution.py:536

commit v6 on v5

--- a/solution.py
+++ b/solution.py
@@ -189,18 +189,20 @@
         hid[j] = (normed * gain_ref[:, columns]).astype(BF16)
         return carry
 
-    lax.fori_loop(0, BLOCKS, normalise, 0)
-
-    def send_hidden(first, width):
+
+    def send_hidden(first, width, fresh):
         columns = pl.ds(first, width)
         copies = []
         for dx, dc in near:
             to_x, to_c = plus(x, dx, NX), plus(c, dc, 2)
+            if fresh:
+                normalise(to_x * 2 + to_c, 0)
             src, dst = hid.at[to_x * 2 + to_c, :, columns], xh.at[me, :, columns]
             copies.append(send(src, dst, place(to_x, yh, to_c, z, yl)))
         return copies
 
-    hidden_a = send_hidden(0, WIDE)
+    hidden_a = send_hidden(0, WIDE, True)
+    normalise(me, 0)
     xh[me] = hid[me]
 
     for copy in loads[1:6]:
@@ -247,7 +249,7 @@
     relay()
     for copy in hidden_a:
         copy.wait_recv()
-    hidden_b = send_hidden(WIDE, PAIR - WIDE)
+    hidden_b = send_hidden(WIDE, PAIR - WIDE, False)
     for k in (1, 3, 2):
         for i in range(3):
             along_y[k, i].wait_recv()

time: 60.2 us -> 60.5 us (level)
  no operation moved by 1% of the time
where the time goes in v6:
time: 60.5 us; the launch traced here: 60.3 us
  Pallas kernels  59.7 us (99%)
  between operations  0.64 us (1%)
    pallas_call x1, Pallas kernels, local(): pl.pallas_call(kernel, out_shape=(pltpu.VMEM((ROWS, QD), BF16), pltpu.VME...  58.4 us
    pallas_call x1, Pallas kernels, local(): pl.pallas_call(hand_over, out_shape=(jax.ShapeDtypeStruct((ROWS, QD), BF1...  1.32 us

profile of v6, /device:TPU:1, one launch (start us, length us, event | category | flops | bytes accessed | tf_op | source)
XLA Modules:
  0.0 60.3 jit_solution(6502073731575093352)
XLA Ops:
  0.6 58.4 %shard_map.119 = (bf16[128,2560]{1,0:T(8,128)(2,1)S(1)}, bf16[128,5120]{1,0:T(8,128)(2,1)S(1)}, f32[16,320]{1,0:T(8,128)S(1)}, f32[8,1,640]{2,1,0:T(1,128)S(1)}, f32[1,512]{1,0:T(1,128)S(1)}) custom-call(bf16[128,5120]{1,0:T(8,128)(2,1)} %x_any.1, bf16[128,2560]{1,0:T(8,128)(2,1)} %q_any.1, bf16[128,512]{1,0:T(8,128)(2,1)} %k_any.1, ...), custom_call_target="tpu_custom_call" | custom-call | tf_op jit(solution)/shard_map/pallas_call | solution.py:488
  59.0 1.3 %shard_map.120 = (bf16[128,2560]{1,0:T(8,128)(2,1)}, bf16[128,5120]{1,0:T(8,128)(2,1)}, f32[16,320]{1,0:T(8,128)}, f32[8,1,640]{2,1,0:T(1,128)}, f32[1,512]{1,0:T(1,128)}) custom-call(bf16[128,2560]{1,0:T(8,128)(2,1)S(1)} %get-tuple-element.15.refs_0_, bf16[128,5120]{1,0:T(8,128)(2,1)S(1)} %get-tuple-element.16.refs_1_, ...), custom_call_target="tpu_custom_call" | custom-call | tf_op jit(solution)/shard_map/pallas_call | solution.py:538
